TPU v7x, 256 devices: a whole 4x4x8 slice. The times are simulated.
256 devices in a mesh: keys: 64 (over y, z, core), seq: 4 (over x).
Axes of the slice: x: 4, y: 4, z: 8, core: 2. Of those that a mesh axis runs over, the one named last changes fastest.
Arguments:
- span_queries: bfloat16 [1536, 768], P(('keys', 'seq')), may hold values from -6 to 6
- key_slab: bfloat16 [4096, 768], P('keys'), may hold values from -0.21875 to 0.21875
- neighbour_store: bfloat16 [4096, 64, 896], P('keys'), may hold values from -6 to 6
- neighbour_ids: int32 [1536, 2], P(('keys', 'seq')), may hold values from 0 to 4094, as said below
- attn_queries: bfloat16 [98304, 2048], P(('keys', 'seq')), may hold values from -200 to 200
- kv_weight: bfloat16 [2, 2048, 896], P(None, 'keys'), may hold values from -0.1875 to 0.1875
Outputs:
- best_scores: float32 [1536, 2], P(('keys', 'seq'))
- attended: bfloat16 [98304, 2048], P(('keys', 'seq'))
Inputs may be any that keep to these rules, and one draw needn't show every extreme that they name: `neighbour_ids`: each id c has c mod 64 at most 62, so c + 1 lies on the same shard c // 64. Among the 12 ids of one device's spans (aligned blocks of 6 rows), no shard holds more than 1, and some shard holds exactly 1.
All inputs are finite; a program needn't handle non-finite values.
Results may differ from a plain program's by a relative error of at most 0.012.
The roundings to bfloat16 on the way count: a program that leaves them out, or rounds other values in their place, can miss the bound.
Values may be sent and summed in bfloat16 or wider, within the bound.
A program may use at most 128 MiB of HBM per device.

v0:
```python
import functools

import jax
import jax.numpy as jnp
import numpy as np
from jax import lax
from jax.experimental import pallas as pl
from jax.experimental.pallas import tpu as pltpu
from jax.sharding import PartitionSpec as P

HEADS = 16
HEAD_DIM = 128
RING_Y, RING_Z, CORES = 4, 8, 2
Y_CAPS = (24, 17)
Z_CAPS = (12, 12, 11, 10)


def key_of(y, z, c):
    return (y * RING_Z + z) * CORES + c


def place():
    k = lax.axis_index("keys")
    return k // (RING_Z * CORES), (k // CORES) % RING_Z, k % CORES


def shifted(dy, dz, dc):
    pairs = []
    for y in range(RING_Y):
        for z in range(RING_Z):
            for c in range(CORES):
                to = key_of((y + dy) % RING_Y, (z + dz) % RING_Z, (c + dc) % CORES)
                pairs.append((key_of(y, z, c), to))
    return pairs


def greet(peers):
    barrier = pltpu.get_barrier_semaphore()
    for peer in peers:
        pl.semaphore_signal(
            barrier, inc=1, device_id={"keys": peer}, device_id_type=pl.DeviceIdType.MESH
        )
    pl.semaphore_wait(barrier, len(peers))


def peer_groups():
    y, z, c = place()
    core = [key_of(y, z, 1 - c)]
    depth = [key_of(y, (z + d) % RING_Z, c) for d in range(1, RING_Z)]
    row = [key_of((y + d) % RING_Y, z, c) for d in range(1, RING_Y)]
    return core, depth, row


def send(src, dst, send_sem, recv_sem, peer):
    copy = pltpu.make_async_remote_copy(
        src_ref=src,
        dst_ref=dst,
        send_sem=send_sem,
        recv_sem=recv_sem,
        device_id={"keys": peer},
        device_id_type=pl.DeviceIdType.MESH,
    )
    copy.start()
    return copy


def gather_ids_kernel(ids_ref, out_ref, held, send_sem, recv_sem):
    y, z, c = place()
    core, depth, row = peer_groups()
    greet(core + depth + row)
    held[y, z, c] = ids_ref[...]
    copies = [send(held.at[y, z, c], held.at[y, z, c], send_sem.at[0], recv_sem.at[0], core[0])]
    for copy in copies:
        copy.wait()
    copies = []
    for i, peer in enumerate(depth):
        copies.append(
            send(held.at[y, z], held.at[y, z], send_sem.at[1 + i], recv_sem.at[1 + i], peer)
        )
    for copy in copies:
        copy.wait()
    copies = []
    for i, peer in enumerate(row):
        copies.append(send(held.at[y], held.at[y], send_sem.at[8 + i], recv_sem.at[8 + i], peer))
    for copy in copies:
        copy.wait()
    out_ref[...] = held[...]


def gather_ids(ids):
    tile = jnp.zeros((8, 128), jnp.int32).at[0, : ids.size].set(ids.reshape(-1))
    shape = (RING_Y, RING_Z, CORES, 8, 128)
    held = pl.pallas_call(
        gather_ids_kernel,
        out_shape=jax.ShapeDtypeStruct(shape, jnp.int32),
        in_specs=[pl.BlockSpec(memory_space=pltpu.VMEM)],
        out_specs=pl.BlockSpec(memory_space=pltpu.VMEM),
        scratch_shapes=[
            pltpu.VMEM(shape, jnp.int32),
            pltpu.SemaphoreType.DMA((11,)),
            pltpu.SemaphoreType.DMA((11,)),
        ],
        compiler_params=pltpu.CompilerParams(collective_id=0, has_side_effects=True),
        name="gather_ids",
    )(tile)
    return held[..., 0, : ids.size].reshape(-1)


def merge(a, b):
    high = jnp.maximum(a[0:1], b[0:1])
    low = jnp.maximum(jnp.minimum(a[0:1], b[0:1]), jnp.maximum(a[1:2], b[1:2]))
    return jnp.concatenate([high, low, jnp.zeros((6, high.shape[1]), high.dtype)], axis=0)


def best_kernel(
    slab_ref, mine_ref, other_ref, out_ref, own, after_core, after_depth, landed, send_sem, recv_sem
):
    core, depth, row = peer_groups()
    greet(core + depth + row)
    c = place()[2]
    for at, queries_ref in ((c, mine_ref), (1 - c, other_ref)):
        count = queries_ref.shape[0]
        scores = lax.dot_general(
            slab_ref[...],
            queries_ref[...],
            (((1,), (1,)), ((), ())),
            preferred_element_type=jnp.float32,
        )
        top = jnp.max(scores, axis=0, keepdims=True)
        at_top = scores == top
        ties = jnp.sum(jnp.where(at_top, 1.0, 0.0), axis=0, keepdims=True)
        rest = jnp.max(jnp.where(at_top, -jnp.inf, scores), axis=0, keepdims=True)
        second = jnp.where(ties > 1.5, top, rest)
        own[:, pl.ds(pl.multiple_of(at * count, count), count)] = jnp.concatenate(
            [top, second, jnp.zeros((6, count), top.dtype)], axis=0
        )
    slot = 0
    holders = [own, after_core, after_depth, out_ref]
    for stage, peers in enumerate((core, depth, row)):
        source = holders[stage]
        copies = []
        for i, peer in enumerate(peers):
            copies.append(
                send(source, landed.at[slot + i], send_sem.at[slot + i], recv_sem.at[slot + i], peer)
            )
        for copy in copies:
            copy.wait()
        total = source[...]
        for i in range(len(peers)):
            total = merge(total, landed[slot + i])
        holders[stage + 1][...] = total
        slot += len(peers)


def best_two(key_slab, mine, other):
    rows = 2 * mine.shape[0]
    return pl.pallas_call(
        best_kernel,
        out_shape=jax.ShapeDtypeStruct((8, rows), jnp.float32),
        in_specs=[pl.BlockSpec(memory_space=pltpu.VMEM)] * 3,
        out_specs=pl.BlockSpec(memory_space=pltpu.VMEM),
        scratch_shapes=[pltpu.VMEM((8, rows), jnp.float32)] * 3
        + [
            pltpu.VMEM((11, 8, rows), jnp.float32),
            pltpu.SemaphoreType.DMA((11,)),
            pltpu.SemaphoreType.DMA((11,)),
        ],
        compiler_params=pltpu.CompilerParams(collective_id=1, has_side_effects=True),
        name="best_two",
    )(key_slab, mine, other)


def take_kernel(counts, reach, row, locs_ref, *refs):
    sources = refs[: len(counts)]
    outs = refs[len(counts) : -1]
    sems = refs[-1]
    starts = np.concatenate([[0], np.cumsum(counts)]).tolist()
    width, rows = outs[0].shape[0], outs[0].shape[1]

    def piece(k, at):
        if sources[k].shape[1] == rows:
            return sources[k].at[at]
        return sources[k].at[at, pl.ds(pl.multiple_of(row(), rows), rows)]

    def begin(s, carry):
        for d, out in enumerate(outs):
            at = locs_ref[d, s]
            for k in reach[d]:

                @pl.when((at >= starts[k]) & (at < starts[k + 1]))
                def _():
                    pltpu.make_async_copy(
                        piece(k, at - starts[k]), out.at[s], sems.at[d, s]
                    ).start()

        return carry

    lax.fori_loop(0, width, begin, 0)

    def finish(s, carry):
        for d, out in enumerate(outs):
            pltpu.make_async_copy(piece(reach[d][0], 0), out.at[s], sems.at[d, s]).wait()
        return carry

    lax.fori_loop(0, width, finish, 0)


def take(sources, reach, locs, rows, row=None):
    counts = tuple(s.shape[0] for s in sources)
    width = locs.shape[1]
    item = (rows, sources[0].shape[2])
    nbytes = 4 * width * item[0] * item[1] * 2
    return pl.pallas_call(
        functools.partial(take_kernel, counts, reach, row),
        out_shape=[jax.ShapeDtypeStruct((width, *item), sources[0].dtype)] * 2,
        in_specs=[pl.BlockSpec(memory_space=pltpu.SMEM)]
        + [pl.BlockSpec(memory_space=pl.ANY)] * len(sources),
        out_specs=[pl.BlockSpec(memory_space=pltpu.VMEM)] * 2,
        scratch_shapes=[pltpu.SemaphoreType.DMA((2, width))],
        cost_estimate=pl.CostEstimate(flops=0, bytes_accessed=nbytes, transcendentals=0),
        compiler_params=pltpu.CompilerParams(vmem_limit_bytes=32 << 20),
        name="take_spans",
    )(locs, *sources)


def attend_kernel(pieces, w_own, w_other, q_ref, o_ref, x, wk, wv):
    c = place()[2]
    parts, requests, part, width = pieces.shape
    spans = requests // 2
    rows = q_ref.shape[0] // spans

    @pl.when(pl.program_id(0) == 0)
    def _():
        for u in range(spans):
            for i in range(parts):
                at = (u * parts + i) * 2 * part
                x[at : at + 2 * part, :] = pieces[i, 2 * u : 2 * u + 2].reshape(2 * part, width)

    for kind, w in enumerate((wk, wv)):
        for j in range(w_own.shape[0]):
            mine = pl.multiple_of(j * 64 + c * 32, 32)
            theirs = pl.multiple_of(j * 64 + (1 - c) * 32, 32)
            w[pl.ds(mine, 32), :] = w_own[j, kind * 32 : kind * 32 + 32, :]
            w[pl.ds(theirs, 32), :] = w_other[j, kind * 32 : kind * 32 + 32, :]
    contract = (((1,), (1,)), ((), ()))
    dot = functools.partial(lax.dot_general, preferred_element_type=jnp.float32)
    for u in range(spans):
        near = x[u * 4 * rows : (u + 1) * 4 * rows, :]
        keys = dot(near, wk[...], contract).astype(jnp.bfloat16)
        values = dot(near, wv[...], contract).astype(jnp.bfloat16)
        for h in range(keys.shape[1] // HEAD_DIM):
            cols = slice(h * HEAD_DIM, (h + 1) * HEAD_DIM)
            q = q_ref[u * rows : (u + 1) * rows, cols]
            logits = dot(q, keys[:, cols], contract) * HEAD_DIM ** (-0.5)
            largest = jnp.max(logits, axis=-1, keepdims=True)
            terms = jnp.exp(logits - largest)
            total = jnp.sum(terms, axis=-1, keepdims=True)
            weights = (terms * (1.0 / total)).astype(jnp.bfloat16)
            out = dot(weights, values[:, cols], (((1,), (0,)), ((), ())))
            o_ref[u * rows : (u + 1) * rows, cols] = out.astype(jnp.bfloat16)


def attend(pieces, w_own, w_other, queries):
    parts, requests, part, width = pieces.shape
    near = requests * parts * part
    tokens, columns = queries.shape
    steps = 8
    pairs = w_own.shape[0] // steps
    cols = columns // steps
    whole = pl.BlockSpec(pieces.shape, lambda g: (0, 0, 0, 0))
    weight = pl.BlockSpec((pairs, w_own.shape[1], width), lambda g: (g, 0, 0))
    block = pl.BlockSpec((tokens, cols), lambda g: (0, g))
    flops = 2 * near * width * 2 * columns
    return pl.pallas_call(
        attend_kernel,
        grid=(steps,),
        out_shape=jax.ShapeDtypeStruct((tokens, columns), jnp.bfloat16),
        in_specs=[whole] + [weight] * 2 + [block],
        out_specs=block,
        scratch_shapes=[
            pltpu.VMEM((near, width), jnp.bfloat16),
            pltpu.VMEM((cols, width), jnp.bfloat16),
            pltpu.VMEM((cols, width), jnp.bfloat16),
        ],
        compiler_params=pltpu.CompilerParams(vmem_limit_bytes=48 << 20),
        cost_estimate=pl.CostEstimate(
            flops=flops, bytes_accessed=20 << 20, transcendentals=tokens * HEADS * 256
        ),
        name="attend",
    )(pieces, w_own, w_other, queries)


def routes(all_ids):
    requests = all_ids.shape[0]
    per_device = requests // (RING_Y * RING_Z * CORES)
    index = np.arange(requests)
    k, n = index // per_device, index % per_device
    to_y, to_z = k // (RING_Z * CORES), (k // CORES) % RING_Z
    tie_y = jnp.asarray((n // 2 + k) % 2 == 1)
    tie_z = jnp.asarray((n + k) % 2 == 1)
    order = jnp.asarray(index, jnp.int32)
    to_y, to_z = jnp.asarray(to_y, jnp.int32), jnp.asarray(to_z, jnp.int32)
    y, z, c = place()
    shard, offset = all_ids // 64, all_ids % 64
    from_y, from_z, from_c = shard // (RING_Z * CORES), (shard // CORES) % RING_Z, shard % CORES
    loc = jnp.where(from_c == c, 0, 64) + offset
    base = 128
    sends = []

    def travel(position, target, ring, tie, node_of, mine, caps, loc, base):
        ahead = (target - position) % ring
        back = (ahead > ring // 2) | ((ahead == ring // 2) & tie)
        left = jnp.where(back, (ring - ahead) % ring, ahead)
        step = jnp.where(back, ring - 1, 1)
        way = back.astype(jnp.int32)
        for width in caps:
            node = node_of(position) * 2 + way
            moving = left > 0
            seat = jnp.where(moving, node, -1)
            priority = (16 - left) * 1024 + order
            before = (seat[:, None] == seat[None, :]) & (priority[:, None] < priority[None, :])
            rank = jnp.sum(before.astype(jnp.int32), axis=0)
            goes = moving & (rank < width)
            seat_rank = jnp.where(goes, node * 64 + rank, -1)
            wanted = (mine * 2 + np.arange(2, dtype=np.int32))[:, None] * 64 + np.arange(
                width, dtype=np.int32
            )
            hit = seat_rank[None, None, :] == wanted[:, :, None]
            sends.append(jnp.sum(jnp.where(hit, loc[None, None, :], 0), axis=-1))
            loc = jnp.where(goes, base + way * width + rank, loc)
            base += 2 * width
            position = jnp.where(goes, (position + step) % ring, position)
            left = left - goes.astype(jnp.int32)
        return jnp.max(left), loc, base

    stuck_y, loc, base = travel(
        from_y, to_y, RING_Y, tie_y, lambda p: p * RING_Z + from_z, y * RING_Z + z, Y_CAPS, loc, base
    )
    stuck_z, loc, base = travel(
        from_z, to_z, RING_Z, tie_z, lambda p: to_y * RING_Z + p, y * RING_Z + z, Z_CAPS, loc, base
    )
    table = loc.reshape(RING_Y * RING_Z, CORES, per_device)
    here = lax.dynamic_index_in_dim(table, y * RING_Z + z, 0, False)
    own = lax.dynamic_index_in_dim(here, c, 0, False)
    other = lax.dynamic_index_in_dim(here, 1 - c, 0, False)
    return sends, jnp.stack([own, other]), jnp.maximum(stuck_y, stuck_z)


def issue_order(moves, widths, chunks):
    done = {(j, -1): 0.0 for j in range(chunks)}
    issued, order, free, clock = set(), [], {True: 0.0, False: 0.0}, 0.0
    while len(order) < chunks * len(moves):
        ready = []
        for j in range(chunks):
            r = sum((j, q) in issued for q in range(len(moves)))
            if r == len(moves) or (j, r - 1) not in done:
                continue
            if r == 0 and j >= 2 and (j - 2, len(Y_CAPS) - 1) not in issued:
                continue
            ready.append((max(clock, done[j, r - 1] + 2.5 * (r > 0)), j, r))
        at, j, r = min(ready)
        along_y = moves[r][0] != 0
        clock = at + 0.5
        free[along_y] = max(free[along_y], clock) + 0.65 * widths[r]
        done[j, r] = free[along_y]
        issued.add((j, r))
        order.append((j, r))
    return order


MOVES = [(1, 0)] * len(Y_CAPS) + [(0, 1)] * len(Z_CAPS)
WIDTHS = Y_CAPS + Z_CAPS
CHUNKS = 4
PART = 16


def carry_kernel(requests, locs_ref, final_ref, store_ref, out_ref, held, *rest):
    rounds = len(MOVES)
    total = CHUNKS * rounds
    out_bufs = rest[:total]
    in_bufs = rest[total : 2 * total]
    last, swap_sems, send_sems, recv_sems = rest[2 * total :]
    y, z, c = place()
    half = held.shape[1]
    spans = store_ref.shape[0]
    steps = [((y + dy) % RING_Y, (z + dz) % RING_Z) for dy, dz in ((1, 0), (-1, 0), (0, 1), (0, -1))]
    near = [key_of(a + 0, b + 0, c) for a, b in steps]
    buddy = key_of(y, z, 1 - c)
    greet(near + [buddy])
    mine = pl.ds(pl.multiple_of(c * half, half), half)
    theirs = pl.ds(pl.multiple_of((1 - c) * half, half), half)
    swap = send(
        store_ref.at[:, theirs], held.at[pl.ds(spans, spans)], swap_sems.at[0], swap_sems.at[1], buddy
    )
    keep = pltpu.make_async_copy(store_ref.at[:, mine], held.at[pl.ds(0, spans)], swap_sems.at[2])
    keep.start()
    swap.wait()
    keep.wait()
    bases = np.concatenate([[2 * spans], 2 * spans + np.cumsum(2 * np.array(WIDTHS))]).tolist()

    def picked(j, r, at):
        step, part = j // 2, j % 2
        rows = slice(part * PART, (part + 1) * PART)
        here = jnp.where(at < 2 * spans, at + step, 0)
        value = held[here, rows, :]
        for q in range(r):
            count = 2 * WIDTHS[q]
            inside = (at >= bases[q]) & (at < bases[q] + count)
            value = jnp.where(inside, in_bufs[j * rounds + q][jnp.where(inside, at - bases[q], 0)], value)
        return value

    flights = {}

    def land(j, r):
        for flight in flights[j, r]:
            flight.wait_recv()

    def issue(j, r):
        if r > 0:
            land(j, r - 1)
        width = WIDTHS[r]
        buf = out_bufs[j * rounds + r]

        def fill(s, carry):
            buf[s] = picked(j, r, locs_ref[r, s])
            return carry

        lax.fori_loop(0, 2 * width, fill, 0)
        flights[j, r] = []
        for d in range(2):
            part = pl.ds(d * width, width)
            k = (j * rounds + r) * 2 + d
            peer = near[d if MOVES[r][0] else 2 + d]
            flights[j, r].append(
                send(buf.at[part], in_bufs[j * rounds + r].at[part], send_sems.at[k], recv_sems.at[k], peer)
            )

    def finish(j):
        land(j, rounds - 1)

        def fill(s, carry):
            out_ref[2 * j, s] = picked(j, rounds, final_ref[0, s])
            last[j, s] = picked(j, rounds, final_ref[1, s])
            return carry

        lax.fori_loop(0, requests, fill, 0)
        k = 2 * total + j
        flights[j, rounds] = [
            send(last.at[j], out_ref.at[2 * j + 1], send_sems.at[k], recv_sems.at[k], buddy)
        ]

    waiting = []
    for j, r in issue_order(MOVES, WIDTHS, CHUNKS):
        issue(j, r)
        if r == rounds - 1:
            waiting.append(j)
        elif waiting:
            finish(waiting.pop(0))
    for j in waiting:
        finish(j)
    for j in range(CHUNKS):
        land(j, rounds)
    for copies in flights.values():
        for copy in copies:
            copy.wait_send()


def carry(store, sends, final):
    spans, rows, enc_width = store.shape
    requests = final.shape[1]
    longest = 2 * max(WIDTHS)
    locs = jnp.stack([jnp.pad(t.reshape(-1), (0, longest - t.size)) for t in sends])
    item = (PART, enc_width)
    bufs = [pltpu.VMEM((2 * w, *item), store.dtype) for _ in range(CHUNKS) for w in WIDTHS]
    copies = 2 * len(bufs) + CHUNKS
    return pl.pallas_call(
        functools.partial(carry_kernel, requests),
        out_shape=jax.ShapeDtypeStruct((2 * CHUNKS, requests, *item), store.dtype),
        in_specs=[pl.BlockSpec(memory_space=pltpu.SMEM)] * 2 + [pl.BlockSpec(memory_space=pl.ANY)],
        out_specs=pl.BlockSpec(memory_space=pltpu.VMEM),
        scratch_shapes=[pltpu.VMEM((2 * spans, rows // 2, enc_width), store.dtype)]
        + bufs * 2
        + [
            pltpu.VMEM((CHUNKS, requests, *item), store.dtype),
            pltpu.SemaphoreType.DMA((3,)),
            pltpu.SemaphoreType.DMA((copies,)),
            pltpu.SemaphoreType.DMA((copies,)),
        ],
        compiler_params=pltpu.CompilerParams(
            collective_id=2, has_side_effects=True, vmem_limit_bytes=60 << 20
        ),
        cost_estimate=pl.CostEstimate(flops=0, bytes_accessed=500 << 20, transcendentals=0),
        name="carry",
    )(locs, final, store)


def direct(neighbour_store, neighbour_ids):
    key_count = lax.axis_size("keys")
    shard_spans = neighbour_store.shape[0]
    flat_ids = neighbour_ids.reshape(-1)
    target, offset = flat_ids // shard_spans, flat_ids % shard_spans
    hit = target[:, None] == jnp.arange(key_count, dtype=jnp.int32)[None, :]
    table = jnp.sum(jnp.where(hit, offset[:, None], 0), axis=0)
    incoming = lax.all_to_all(table, "keys", split_axis=0, concat_axis=0, tiled=True)
    firsts, seconds = take(
        [neighbour_store], [[0]] * 2, jnp.stack([incoming, incoming + 1]), neighbour_store.shape[1]
    )
    arrived = [
        lax.all_to_all(spans, "keys", split_axis=0, concat_axis=0, tiled=True)
        for spans in (firsts, seconds)
    ]
    locs = jnp.stack([target, key_count + target])
    return take(arrived, [[0], [1]], locs, neighbour_store.shape[1])


def body(span_queries, key_slab, neighbour_store, neighbour_ids, attn_queries, kv_weight):
    position = lax.axis_index("keys")
    y, z, c = place()
    own_spans = neighbour_ids.shape[0]
    span_rows = neighbour_store.shape[1]
    enc_width = neighbour_store.shape[2]
    all_ids = gather_ids(neighbour_ids)
    asked = jnp.zeros((16, enc_width), span_queries.dtype)
    asked = lax.dynamic_update_slice(asked, span_queries, (0, 0))
    shard = jnp.concatenate([kv_weight[0], kv_weight[1], asked], axis=0)
    groups = [[key_of(a, b, d) for a in range(RING_Y) for b in range(RING_Z)] for d in range(CORES)]
    weight_own = lax.all_gather(shard, "keys", axis=0, axis_index_groups=groups)
    weight_other = lax.ppermute(weight_own, "keys", shifted(0, 0, 1))
    sends, final, stuck = routes(all_ids)
    flag = jnp.full((8, 128), stuck, jnp.int32)
    seq = lax.axis_size("seq")
    worst = flag
    for d in range(1, seq):
        worst = jnp.maximum(
            worst, lax.ppermute(flag, "seq", [(s, (s + d) % seq) for s in range(seq)])
        )
    pieces = carry(neighbour_store, sends, final)

    def resend(store, ids, fast):
        return jnp.stack(
            [
                spans[:, h * PART : (h + 1) * PART]
                for spans in direct(store, ids)
                for h in range(span_rows // PART)
            ]
        )

    pieces = lax.cond(
        worst[0, 0] > 0, resend, lambda store, ids, fast: fast, neighbour_store, neighbour_ids, pieces
    )
    asked_rows = [
        w[:, -16:, : span_queries.shape[1]].reshape(-1, span_queries.shape[1])
        for w in (weight_own, weight_other)
    ]
    best = best_two(key_slab, *asked_rows)
    column = c * asked_rows[0].shape[0] + (position // CORES) * 16
    best_scores = lax.dynamic_slice_in_dim(best, column, own_spans, axis=1)[:2].T
    attended = attend(pieces, weight_own, weight_other, attn_queries)
    return (best_scores, attended)


def solution(mesh):
    return jax.shard_map(
        body,
        mesh=mesh,
        in_specs=(
            P(("keys", "seq"), None),
            P("keys", None),
            P("keys", None, None),
            P(("keys", "seq"), None),
            P(("keys", "seq"), None),
            P(None, "keys", None),
        ),
        out_specs=(P(("keys", "seq"), None), P(("keys", "seq"), None)),
        check_vma=False,
    )
```

profile of v0, /device:TPU:1, one launch (start us, length us, event | category | flops | bytes accessed | tf_op | source)
XLA Modules:
  0.0 375.6 jit_solution(4783823021167460708)
XLA Ops:
  7.2 0.9 slice_bitcast_fusion.1
  8.1 1.4 fusion.1
  9.5 0.8 copy.36
  10.3 0.6 scatter.4.ids_ref
  10.9 20.2 %gather_ids.1 = s32[4,8,2,8,128]{4,3,2,1,0:T(8,128)} custom-call(s32[8,128]{1,0:T(8,128)} %scatter.4.ids_ref), custom_call_target="tpu_custom_call" | custom-call | tf_op jit(solution)/shard_map/gather_ids/pallas_call | solution.py:93
  31.1 1.1 slice_reduce_fusion
  32.2 0.1 reshape_squeeze.3
  32.3 0.8 fusion.38
  33.1 0.5 convert_reduce_fusion.3
  33.5 0.7 add_select_fusion.20
  34.2 0.8 fusion.39
  35.0 0.5 convert_reduce_fusion.5
  35.5 0.5 convert_reduce_fusion.2
  35.9 59.5 %all-gather.3.cloned.1.call-done = bf16[2560,896]{1,0:T(8,128)(2,1)} async-done(((bf16[80,896]{1,0:T(8,128)(2,1)}), bf16[2560,896]{1,0:T(8,128)(2,1)}) %all-gather.3.cloned.1.call-update) | async-done | bytes 4587536 | tf_op jit(solution)/shard_map/all_gather | solution.py:527
  95.4 3.4 collective-permute-start
  98.9 0.8 add_select_fusion.18
  99.6 0.8 broadcast_select_fusion.1
  100.4 0.5 convert_reduce_fusion.4
  100.8 0.6 subtract_reduce_fusion.1
  101.5 0.5 convert_reduce_fusion.1
  101.9 0.7 add_select_fusion.17
  102.6 0.7 broadcast_select_fusion
  103.3 0.5 convert_reduce_fusion
  103.8 1.4 add_select_fusion.14
  106.5 1.3 collective-permute-start.1
  107.8 2.4 collective-permute-start.2
  110.2 1.2 collective-permute-start.3
  111.3 0.1 reshape.495
  111.5 0.4 fusion.5
  111.9 0.1 copy.40
  112.0 0.7 add_select_fusion.16
  112.8 0.3 fusion.6
  113.1 0.1 copy.41
  113.3 0.6 fusion.4
  114.2 0.5 fusion.2
  114.8 0.6 pad_add_fusion.2.final_ref
  115.5 0.2 select_reduce_fusion.1
  115.8 0.6 stack.71.locs_ref
  116.4 180.1 %carry.1 = bf16[8,12,16,896]{3,2,1,0:T(8,128)(2,1)} custom-call(s32[6,48]{1,0:T(8,128)} %stack.71.locs_ref, s32[2,12]{1,0:T(2,128)} %pad_add_fusion.2.final_ref, bf16[64,64,896]{2,1,0:T(8,128)(2,1)} %store_ref.1), custom_call_target="tpu_custom_call" | custom-call | bytes 524288000 | tf_op jit(solution)/shard_map/carry/pallas_call | solution.py:476
  296.6 0.5 slice.67
  297.8 0.2 conditional.1
  298.0 2.2 slice.68
  300.2 2.1 slice.69
  302.2 19.4 %best_two.1 = f32[8,1024]{1,0:T(8,128)} custom-call(bf16[64,768]{1,0:T(8,128)(2,1)} %slab_ref.1, bf16[512,768]{1,0:T(8,128)(2,1)} %bitcast.46, bf16[512,768]{1,0:T(8,128)(2,1)} %bitcast.47), custom_call_target="tpu_custom_call" | custom-call | tf_op jit(solution)/shard_map/best_two/pallas_call | solution.py:157
  321.6 0.8 constant_dynamic-slice_fusion.2
  322.4 0.6 slice_bitcast_fusion.2
  323.0 2.3 copy-done.2
  325.3 43.5 %attend.1 = bf16[384,2048]{1,0:T(8,128)(2,1)} custom-call(bf16[8,12,16,896]{3,2,1,0:T(8,128)(2,1)} %get-tuple-element.99.pieces, bf16[32,80,896]{2,1,0:T(8,128)(2,1)S(1)} %bitcast.45, bf16[32,80,896]{2,1,0:T(8,128)(2,1)} %collective-permute-done.w_other, bf16[384,2048]{1,0:T(8,128)(2,1)S(1)} %copy-done.3), custom_call_target="tpu_custom_call" | custom-call | flops 11274289152 | bytes 20971520 | tf_op jit(solution)/shard_map/attend/pallas_call | solution.py:274
  (35 shorter events, 1.1 us)
Async XLA Ops:
  7.2 88.3 %all-gather.3.cloned.1.call-start = ((), (), s32[]{:S(2)}) async-start(), calls=%async_computation.3 | async-start | bytes 4730880 | tf_op jit(solution)/shard_map/all_gather | solution.py:527
  95.4 204.7 %collective-permute-start = (bf16[32,80,896]{2,1,0:T(8,128)(2,1)}, bf16[32,80,896]{2,1,0:T(8,128)(2,1)}, u32[]{:S(2)}, u32[]{:S(2)}) collective-permute-start(bf16[32,80,896]{2,1,0:T(8,128)(2,1)} %bitcast.43), channel_id=1, source_target_pairs={{0,4},{4,0},{8,12},{12,8},{16,20},{20,16},{24,28},{28,24},{32,36},... | collective-permute-start | bytes 13762568 | tf_op jit(solution)/shard_map/ppermute | solution.py:528
  106.5 190.0 %collective-permute-start.1 = (s32[8,128]{1,0:T(8,128)S(1)}, s32[8,128]{1,0:T(8,128)S(1)}, u32[]{:S(2)}, u32[]{:S(2)}) collective-permute-start(s32[8,128]{1,0:T(8,128)S(1)} %broadcast_in_dim.93), channel_id=1, source_target_pairs={{0,1},{1,2},{2,3},{3,0},{4,5},{5,6},{6,7},{7,4},{8,9},{9,10},{10,1... | collective-permute-start | bytes 12296 | tf_op jit(solution)/shard_map/ppermute | solution.py:535
  107.8 188.8 %collective-permute-start.2 = (s32[8,128]{1,0:T(8,128)S(1)}, s32[8,128]{1,0:T(8,128)S(1)}, u32[]{:S(2)}, u32[]{:S(2)}) collective-permute-start(s32[8,128]{1,0:T(8,128)S(1)} %broadcast_in_dim.93), channel_id=1, source_target_pairs={{0,2},{1,3},{2,0},{3,1},{4,6},{5,7},{6,4},{7,5},{8,10},{9,11},{10,... | collective-permute-start | bytes 12296 | tf_op jit(solution)/shard_map/ppermute | solution.py:535
  110.2 186.4 %collective-permute-start.3 = (s32[8,128]{1,0:T(8,128)S(1)}, s32[8,128]{1,0:T(8,128)S(1)}, u32[]{:S(2)}, u32[]{:S(2)}) collective-permute-start(s32[8,128]{1,0:T(8,128)S(1)} %broadcast_in_dim.93), channel_id=1, source_target_pairs={{0,3},{1,0},{2,1},{3,2},{4,7},{5,4},{6,5},{7,6},{8,11},{9,8},{10,9... | collective-permute-start | bytes 12296 | tf_op jit(solution)/shard_map/ppermute | solution.py:535
  116.4 181.4 %copy-start.4 = (s32[6,2]{0,1:T(2,128)S(1)}, s32[6,2]{0,1:T(2,128)}, u32[]{:S(2)}) copy-start(s32[6,2]{0,1:T(2,128)} %param.30) | copy-start | bytes 148
  297.9 25.0 %copy-start.3 = (bf16[384,2048]{1,0:T(8,128)(2,1)S(1)}, bf16[384,2048]{1,0:T(8,128)(2,1)}, u32[]{:S(2)}) copy-start(bf16[384,2048]{1,0:T(8,128)(2,1)} %q_ref.1) | copy-start | bytes 4718596
  323.0 2.3 copy-start.2
Sparse Core Ops, SparseCore 0:
  11.2 84.2 all-gather.2
where the time goes:
time: 376 us
  Pallas kernels  263 us (70%)
  waiting for transfers between devices  59.5 us (16%)
  between operations  16.2 us (4%)
  other arithmetic  14.6 us (4%)
  local copies, waits for them, and re-layouts  13.6 us (4%)
  starting transfers between devices  8.3 us (2%)
    pallas_call x1, Pallas kernels, carry(): pl.pallas_call(functools.partial(carry_kernel, requests), out_shape=jax.S...  180 us
    all_gather x1, waiting for transfers between devices, body(): weight_own = lax.all_gather(shard, 'keys', axis=0, axis_index_groups=groups)  59.5 us
    pallas_call x1, Pallas kernels, attend(): pl.pallas_call(attend_kernel, grid=(steps,), out_shape=jax.ShapeDtypeStru...  43.5 us
    pallas_call x1, Pallas kernels, gather_ids(): pl.pallas_call(gather_ids_kernel, out_shape=jax.ShapeDtypeStruct(shape, j...  20.2 us
    pallas_call x1, Pallas kernels, best_two(): pl.pallas_call(best_kernel, out_shape=jax.ShapeDtypeStruct((8, rows), jnp...  19.4 us
  transfers between devices with their start and end apart: 5, of which 1 were waited for; matrix products, arithmetic and copies ran while one was open for 5% of the time, Pallas kernels for 53%

commit v1 on v0

--- a/solution.py
+++ b/solution.py
@@ -112,64 +112,6 @@
     return jnp.concatenate([high, low, jnp.zeros((6, high.shape[1]), high.dtype)], axis=0)
 
 
-def best_kernel(
-    slab_ref, mine_ref, other_ref, out_ref, own, after_core, after_depth, landed, send_sem, recv_sem
-):
-    core, depth, row = peer_groups()
-    greet(core + depth + row)
-    c = place()[2]
-    for at, queries_ref in ((c, mine_ref), (1 - c, other_ref)):
-        count = queries_ref.shape[0]
-        scores = lax.dot_general(
-            slab_ref[...],
-            queries_ref[...],
-            (((1,), (1,)), ((), ())),
-            preferred_element_type=jnp.float32,
-        )
-        top = jnp.max(scores, axis=0, keepdims=True)
-        at_top = scores == top
-        ties = jnp.sum(jnp.where(at_top, 1.0, 0.0), axis=0, keepdims=True)
-        rest = jnp.max(jnp.where(at_top, -jnp.inf, scores), axis=0, keepdims=True)
-        second = jnp.where(ties > 1.5, top, rest)
-        own[:, pl.ds(pl.multiple_of(at * count, count), count)] = jnp.concatenate(
-            [top, second, jnp.zeros((6, count), top.dtype)], axis=0
-        )
-    slot = 0
-    holders = [own, after_core, after_depth, out_ref]
-    for stage, peers in enumerate((core, depth, row)):
-        source = holders[stage]
-        copies = []
-        for i, peer in enumerate(peers):
-            copies.append(
-                send(source, landed.at[slot + i], send_sem.at[slot + i], recv_sem.at[slot + i], peer)
-            )
-        for copy in copies:
-            copy.wait()
-        total = source[...]
-        for i in range(len(peers)):
-            total = merge(total, landed[slot + i])
-        holders[stage + 1][...] = total
-        slot += len(peers)
-
-
-def best_two(key_slab, mine, other):
-    rows = 2 * mine.shape[0]
-    return pl.pallas_call(
-        best_kernel,
-        out_shape=jax.ShapeDtypeStruct((8, rows), jnp.float32),
-        in_specs=[pl.BlockSpec(memory_space=pltpu.VMEM)] * 3,
-        out_specs=pl.BlockSpec(memory_space=pltpu.VMEM),
-        scratch_shapes=[pltpu.VMEM((8, rows), jnp.float32)] * 3
-        + [
-            pltpu.VMEM((11, 8, rows), jnp.float32),
-            pltpu.SemaphoreType.DMA((11,)),
-            pltpu.SemaphoreType.DMA((11,)),
-        ],
-        compiler_params=pltpu.CompilerParams(collective_id=1, has_side_effects=True),
-        name="best_two",
-    )(key_slab, mine, other)
-
-
 def take_kernel(counts, reach, row, locs_ref, *refs):
     sources = refs[: len(counts)]
     outs = refs[len(counts) : -1]
@@ -223,71 +165,216 @@
     )(locs, *sources)
 
 
-def attend_kernel(pieces, w_own, w_other, q_ref, o_ref, x, wk, wv):
+def top_two(scores):
+    top = jnp.max(scores, axis=0, keepdims=True)
+    at_top = scores == top
+    ties = jnp.sum(jnp.where(at_top, 1.0, 0.0), axis=0, keepdims=True)
+    rest = jnp.max(jnp.where(at_top, -jnp.inf, scores), axis=0, keepdims=True)
+    second = jnp.where(ties > 1.5, top, rest)
+    return jnp.concatenate([top, second, jnp.zeros((6, top.shape[1]), top.dtype)], axis=0)
+
+
+SWAP, SLAB, DEPTH, ROW = 0, 8, 9, 16
+
+
+def attend_kernel(
+    pieces,
+    w_own,
+    w_all,
+    slab,
+    q_ref,
+    o_ref,
+    best_ref,
+    x,
+    wk,
+    wv,
+    keys,
+    values,
+    w_other,
+    other_slab,
+    asked,
+    found,
+    after_depth,
+    landed,
+    asked_sem,
+    send_sem,
+    recv_sem,
+):
     c = place()[2]
+    g = pl.program_id(0)
     parts, requests, part, width = pieces.shape
     spans = requests // 2
+    near = 2 * part * parts
     rows = q_ref.shape[0] // spans
-
-    @pl.when(pl.program_id(0) == 0)
+    pairs = w_own.shape[0]
+    steps = w_all.shape[0] // pairs
+    core, depth, row = peer_groups()
+    contract = (((1,), (1,)), ((), ()))
+    dot = functools.partial(lax.dot_general, preferred_element_type=jnp.float32)
+
+    def flight(src, dst, k, peer):
+        return pltpu.make_async_remote_copy(
+            src_ref=src,
+            dst_ref=dst,
+            send_sem=send_sem.at[k],
+            recv_sem=recv_sem.at[k],
+            device_id={"keys": peer},
+            device_id_type=pl.DeviceIdType.MESH,
+        )
+
+    def weights_flight(b):
+        at = pl.ds(b * pairs, pairs)
+        return flight(w_all.at[at, pl.ds(0, 64)], w_other.at[at], SWAP + b, core[0])
+
+    slab_flight = lambda: flight(slab, other_slab, SLAB, core[0])
+    asked_copy = lambda: pltpu.make_async_copy(w_all.at[:, pl.ds(64, 16)], asked, asked_sem)
+    depth_flights = lambda: [
+        flight(found, landed.at[i], DEPTH + i, peer) for i, peer in enumerate(depth)
+    ]
+    row_flights = lambda: [
+        flight(after_depth, landed.at[len(depth) + i], ROW + i, peer) for i, peer in enumerate(row)
+    ]
+
+    @pl.when(g == 0)
     def _():
+        greet(core + depth + row)
+        for b in range(steps):
+            weights_flight(b).start()
+        slab_flight().start()
+        asked_copy().start()
         for u in range(spans):
             for i in range(parts):
                 at = (u * parts + i) * 2 * part
                 x[at : at + 2 * part, :] = pieces[i, 2 * u : 2 * u + 2].reshape(2 * part, width)
 
+    weights_flight(g).wait_recv()
     for kind, w in enumerate((wk, wv)):
-        for j in range(w_own.shape[0]):
+        for j in range(pairs):
             mine = pl.multiple_of(j * 64 + c * 32, 32)
             theirs = pl.multiple_of(j * 64 + (1 - c) * 32, 32)
             w[pl.ds(mine, 32), :] = w_own[j, kind * 32 : kind * 32 + 32, :]
-            w[pl.ds(theirs, 32), :] = w_other[j, kind * 32 : kind * 32 + 32, :]
-    contract = (((1,), (1,)), ((), ()))
-    dot = functools.partial(lax.dot_general, preferred_element_type=jnp.float32)
-    for u in range(spans):
-        near = x[u * 4 * rows : (u + 1) * 4 * rows, :]
-        keys = dot(near, wk[...], contract).astype(jnp.bfloat16)
-        values = dot(near, wv[...], contract).astype(jnp.bfloat16)
-        for h in range(keys.shape[1] // HEAD_DIM):
-            cols = slice(h * HEAD_DIM, (h + 1) * HEAD_DIM)
-            q = q_ref[u * rows : (u + 1) * rows, cols]
-            logits = dot(q, keys[:, cols], contract) * HEAD_DIM ** (-0.5)
-            largest = jnp.max(logits, axis=-1, keepdims=True)
-            terms = jnp.exp(logits - largest)
-            total = jnp.sum(terms, axis=-1, keepdims=True)
-            weights = (terms * (1.0 / total)).astype(jnp.bfloat16)
-            out = dot(weights, values[:, cols], (((1,), (0,)), ((), ())))
-            o_ref[u * rows : (u + 1) * rows, cols] = out.astype(jnp.bfloat16)
-
-
-def attend(pieces, w_own, w_other, queries):
+            w[pl.ds(theirs, 32), :] = w_other[g * pairs + j, kind * 32 : kind * 32 + 32, :]
+    keys[...] = dot(x[...], wk[...], contract).astype(jnp.bfloat16)
+    values[...] = dot(x[...], wv[...], contract).astype(jnp.bfloat16)
+    zero = jnp.zeros((rows, HEAD_DIM), jnp.bfloat16)
+
+    def both_heads(u):
+        q = q_ref[u * rows : (u + 1) * rows, :]
+        return jnp.concatenate(
+            [
+                jnp.concatenate([q[:, :HEAD_DIM], zero], axis=1),
+                jnp.concatenate([zero, q[:, HEAD_DIM:]], axis=1),
+            ],
+            axis=0,
+        )
+
+    def softmax(logits):
+        scaled = logits * HEAD_DIM ** (-0.5)
+        largest = jnp.max(scaled, axis=-1, keepdims=True)
+        terms = jnp.exp(scaled - largest)
+        total = jnp.sum(terms, axis=-1, keepdims=True)
+        return (terms * (1.0 / total)).astype(jnp.bfloat16)
+
+    logits = [dot(both_heads(u), keys[u * near : (u + 1) * near, :], contract) for u in range(spans)]
+    weights = [softmax(part_logits) for part_logits in logits]
+    outs = [
+        dot(weights[u], values[u * near : (u + 1) * near, :], (((1,), (0,)), ((), ())))
+        for u in range(spans)
+    ]
+    for u, out in enumerate(outs):
+        tokens = slice(u * rows, (u + 1) * rows)
+        o_ref[tokens, :HEAD_DIM] = out[:rows, :HEAD_DIM].astype(jnp.bfloat16)
+        o_ref[tokens, HEAD_DIM:] = out[rows:, HEAD_DIM:].astype(jnp.bfloat16)
+
+    @pl.when(g == 1)
+    def _():
+        slab_flight().wait_recv()
+        asked_copy().wait()
+        queries = asked[:, :, : slab.shape[1]].reshape(found.shape[1], slab.shape[1])
+        found[...] = merge(
+            top_two(dot(slab[...], queries, contract)), top_two(dot(other_slab[...], queries, contract))
+        )
+        for copy in depth_flights():
+            copy.start()
+
+    @pl.when(g == 3)
+    def _():
+        for copy in depth_flights():
+            copy.wait_recv()
+        total = found[...]
+        for i in range(len(depth)):
+            total = merge(total, landed[i])
+        after_depth[...] = total
+        for copy in row_flights():
+            copy.start()
+
+    @pl.when(g == 5)
+    def _():
+        for copy in row_flights():
+            copy.wait_recv()
+        total = after_depth[...]
+        for i in range(len(row)):
+            total = merge(total, landed[len(depth) + i])
+        best_ref[...] = total
+
+    @pl.when(g == steps - 1)
+    def _():
+        for b in range(steps):
+            weights_flight(b).wait_send()
+        for copy in [slab_flight()] + depth_flights() + row_flights():
+            copy.wait_send()
+
+
+def attend(pieces, w_own, slab, queries):
     parts, requests, part, width = pieces.shape
     near = requests * parts * part
     tokens, columns = queries.shape
     steps = 8
     pairs = w_own.shape[0] // steps
     cols = columns // steps
-    whole = pl.BlockSpec(pieces.shape, lambda g: (0, 0, 0, 0))
-    weight = pl.BlockSpec((pairs, w_own.shape[1], width), lambda g: (g, 0, 0))
+    asked = w_own.shape[0] * 16
     block = pl.BlockSpec((tokens, cols), lambda g: (0, g))
     flops = 2 * near * width * 2 * columns
+    bf16 = jnp.bfloat16
     return pl.pallas_call(
         attend_kernel,
         grid=(steps,),
-        out_shape=jax.ShapeDtypeStruct((tokens, columns), jnp.bfloat16),
-        in_specs=[whole] + [weight] * 2 + [block],
-        out_specs=block,
+        out_shape=[
+            jax.ShapeDtypeStruct((tokens, columns), bf16),
+            jax.ShapeDtypeStruct((8, asked), jnp.float32),
+        ],
+        in_specs=[
+            pl.BlockSpec(pieces.shape, lambda g: (0, 0, 0, 0)),
+            pl.BlockSpec((pairs, w_own.shape[1], width), lambda g: (g, 0, 0)),
+            pl.BlockSpec(memory_space=pl.ANY),
+            pl.BlockSpec(slab.shape, lambda g: (0, 0)),
+            block,
+        ],
+        out_specs=[block, pl.BlockSpec((8, asked), lambda g: (0, 0))],
         scratch_shapes=[
-            pltpu.VMEM((near, width), jnp.bfloat16),
-            pltpu.VMEM((cols, width), jnp.bfloat16),
-            pltpu.VMEM((cols, width), jnp.bfloat16),
+            pltpu.VMEM((near, width), bf16),
+            pltpu.VMEM((cols, width), bf16),
+            pltpu.VMEM((cols, width), bf16),
+            pltpu.VMEM((near, cols), bf16),
+            pltpu.VMEM((near, cols), bf16),
+            pltpu.VMEM((w_own.shape[0], 64, width), bf16),
+            pltpu.VMEM(slab.shape, bf16),
+            pltpu.VMEM((w_own.shape[0], 16, width), bf16),
+            pltpu.VMEM((8, asked), jnp.float32),
+            pltpu.VMEM((8, asked), jnp.float32),
+            pltpu.VMEM((10, 8, asked), jnp.float32),
+            pltpu.SemaphoreType.DMA,
+            pltpu.SemaphoreType.DMA((19,)),
+            pltpu.SemaphoreType.DMA((19,)),
         ],
-        compiler_params=pltpu.CompilerParams(vmem_limit_bytes=48 << 20),
+        compiler_params=pltpu.CompilerParams(
+            collective_id=1, has_side_effects=True, vmem_limit_bytes=48 << 20
+        ),
         cost_estimate=pl.CostEstimate(
             flops=flops, bytes_accessed=20 << 20, transcendentals=tokens * HEADS * 256
         ),
         name="attend",
-    )(pieces, w_own, w_other, queries)
+    )(pieces, w_own, w_own, slab, queries)
 
 
 def routes(all_ids):
@@ -525,7 +612,6 @@
     shard = jnp.concatenate([kv_weight[0], kv_weight[1], asked], axis=0)
     groups = [[key_of(a, b, d) for a in range(RING_Y) for b in range(RING_Z)] for d in range(CORES)]
     weight_own = lax.all_gather(shard, "keys", axis=0, axis_index_groups=groups)
-    weight_other = lax.ppermute(weight_own, "keys", shifted(0, 0, 1))
     sends, final, stuck = routes(all_ids)
     flag = jnp.full((8, 128), stuck, jnp.int32)
     seq = lax.axis_size("seq")
@@ -548,14 +634,9 @@
     pieces = lax.cond(
         worst[0, 0] > 0, resend, lambda store, ids, fast: fast, neighbour_store, neighbour_ids, pieces
     )
-    asked_rows = [
-        w[:, -16:, : span_queries.shape[1]].reshape(-1, span_queries.shape[1])
-        for w in (weight_own, weight_other)
-    ]
-    best = best_two(key_slab, *asked_rows)
-    column = c * asked_rows[0].shape[0] + (position // CORES) * 16
+    attended, best = attend(pieces, weight_own, key_slab, attn_queries)
+    column = (position // CORES) * 16
     best_scores = lax.dynamic_slice_in_dim(best, column, own_spans, axis=1)[:2].T
-    attended = attend(pieces, weight_own, weight_other, attn_queries)
     return (best_scores, attended)
 
 

time: 376 us -> 294 us (0.78)
  waiting for transfers between devices: 59.5 us -> 0.05 us
  Pallas kernels: 263 us -> 250 us
  local copies, waits for them, and re-layouts: 13.6 us -> 8.66 us
  starting transfers between devices: 8.3 us -> 3.72 us
    all_gather x1, waiting for transfers between devices: 59.5 us -> 0.02 us  [body(): weight_own = lax.all_gather(shard, 'keys', axis=0, axis_index_groups=groups)]
    pallas_call x2 -> x1, Pallas kernels: 62.9 us -> 29.3 us  [attend(): pl.pallas_call(attend_kernel, grid=(steps,), out_shape=[jax.ShapeDtypeStr...]
    pallas_call x1, Pallas kernels: 180 us -> 200 us  [carry(): pl.pallas_call(functools.partial(carry_kernel, requests), out_shape=jax.S...]
    slice x2 -> x0, local copies, waits for them, and re-layouts: 4.26 us -> none  [body(): w[:, -16:, :span_queries.shape[1]].reshape(-1, span_queries.shape[1])]
  transfers between devices with their start and end apart: 5 -> 4, of which waited for: 1 -> 0; matrix products, arithmetic and copies ran while one was open for 5% -> 6% of each run, Pallas kernels for 53% -> 75%
where the time goes in v1:
time: 294 us; the launch traced here: 293 us
  Pallas kernels  250 us (85%)
  between operations  16.3 us (6%)
  other arithmetic  14.6 us (5%)
  local copies, waits for them, and re-layouts  8.66 us (3%)
  starting transfers between devices  3.72 us (1%)
    pallas_call x1, Pallas kernels, carry(): pl.pallas_call(functools.partial(carry_kernel, requests), out_shape=jax.S...  200 us
    pallas_call x1, Pallas kernels, attend(): pl.pallas_call(attend_kernel, grid=(steps,), out_shape=[jax.ShapeDtypeStr...  29.3 us
    pallas_call x1, Pallas kernels, gather_ids(): pl.pallas_call(gather_ids_kernel, out_shape=jax.ShapeDtypeStruct(shape, j...  20.2 us
  transfers between devices with their start and end apart: 4, of which 0 were waited for; matrix products, arithmetic and copies ran while one was open for 6% of the time, Pallas kernels for 75%

profile of v1, /device:TPU:1, one launch (start us, length us, event | category | flops | bytes accessed | tf_op | source)
XLA Modules:
  0.0 293.2 jit_solution(5349681901248795827)
XLA Ops:
  7.2 0.9 slice_bitcast_fusion.1
  8.1 1.4 fusion.1
  9.5 0.8 copy.36
  10.3 0.6 scatter.4.ids_ref
  10.9 20.2 %gather_ids.1 = s32[4,8,2,8,128]{4,3,2,1,0:T(8,128)} custom-call(s32[8,128]{1,0:T(8,128)} %scatter.4.ids_ref), custom_call_target="tpu_custom_call" | custom-call | tf_op jit(solution)/shard_map/gather_ids/pallas_call | solution.py:93
  31.1 1.1 slice_reduce_fusion
  32.2 0.1 reshape_squeeze.3
  32.3 0.8 fusion.38
  33.1 0.5 convert_reduce_fusion.3
  33.5 0.7 add_select_fusion.20
  34.2 0.8 fusion.39
  35.0 0.5 convert_reduce_fusion.2
  35.5 0.5 convert_reduce_fusion.5
  35.9 0.8 add_select_fusion.18
  36.7 0.8 broadcast_select_fusion.1
  37.4 0.5 convert_reduce_fusion.4
  37.9 0.6 subtract_reduce_fusion.1
  38.5 0.5 convert_reduce_fusion.1
  39.0 0.7 add_select_fusion.17
  39.7 0.7 broadcast_select_fusion
  40.4 0.5 convert_reduce_fusion
  40.9 1.5 add_select_fusion.14
  43.7 2.6 collective-permute-start.2
  46.2 0.5 collective-permute-start.1
  46.8 0.6 collective-permute-start
  47.4 0.5 fusion.2
  47.8 0.1 copy.37
  47.9 0.1 reshape.482
  48.0 0.6 fusion.4
  48.6 0.1 copy.39
  48.8 0.1 copy.38
  48.9 0.7 add_select_fusion.16
  49.6 0.3 fusion.6
  50.0 0.1 copy.41
  50.1 0.1 reshape.486
  50.2 0.4 fusion.5
  50.5 0.1 copy.40
  50.7 0.1 reshape.487
  50.9 0.6 pad_add_fusion.2.final_ref
  51.5 0.2 select_reduce_fusion.1
  51.8 0.6 stack.71.locs_ref
  52.4 200.1 %carry.1 = bf16[8,12,16,896]{3,2,1,0:T(8,128)(2,1)} custom-call(s32[6,48]{1,0:T(8,128)} %stack.71.locs_ref, s32[2,12]{1,0:T(2,128)} %pad_add_fusion.2.final_ref, bf16[64,64,896]{2,1,0:T(8,128)(2,1)} %store_ref.1), custom_call_target="tpu_custom_call" | custom-call | bytes 524288000 | tf_op jit(solution)/shard_map/carry/pallas_call | solution.py:563
  252.6 0.5 slice.56
  253.8 0.2 conditional.1
  254.1 1.2 copy-done.2
  255.2 29.3 %attend.1 = (bf16[384,2048]{1,0:T(8,128)(2,1)S(1)}, f32[8,512]{1,0:T(8,128)S(1)}) custom-call(bf16[8,12,16,896]{3,2,1,0:T(8,128)(2,1)} %get-tuple-element.107.pieces, bf16[32,80,896]{2,1,0:T(8,128)(2,1)} %bitcast.43, bf16[32,80,896]{2,1,0:T(8,128)(2,1)} %bitcast.44, bf16[64,768]{1,0:T(8,128)(2,1)S(1)} %copy-done.3, bf16[384,2048]{1,0:T(8,128)(2,1)S(1)} %copy-done.2), custom_call_target="tpu_custom_call" | custom-call | flops 11274289152 | bytes 20971520 | tf_op jit(solution)/shard_map/attend/pallas_call | solution.py:339
  284.6 0.6 slice_bitcast_fusion.2
  285.2 1.1 copy.53
  (31 shorter events, 0.7 us)
Async XLA Ops:
  7.2 246.9 %all-gather.3.cloned.1.call-start = ((), (), s32[]{:S(2)}) async-start(), calls=%async_computation.3 | async-start | bytes 4730880 | tf_op jit(solution)/shard_map/all_gather | solution.py:614
  43.7 208.9 %collective-permute-start.2 = (s32[8,128]{1,0:T(8,128)S(1)}, s32[8,128]{1,0:T(8,128)S(1)}, u32[]{:S(2)}, u32[]{:S(2)}) collective-permute-start(s32[8,128]{1,0:T(8,128)S(1)} %broadcast_in_dim.93), channel_id=1, source_target_pairs={{0,3},{1,0},{2,1},{3,2},{4,7},{5,4},{6,5},{7,6},{8,11},{9,8},{10,9... | collective-permute-start | bytes 12296 | tf_op jit(solution)/shard_map/ppermute | solution.py:621
  46.2 206.4 %collective-permute-start.1 = (s32[8,128]{1,0:T(8,128)S(1)}, s32[8,128]{1,0:T(8,128)S(1)}, u32[]{:S(2)}, u32[]{:S(2)}) collective-permute-start(s32[8,128]{1,0:T(8,128)S(1)} %broadcast_in_dim.93), channel_id=1, source_target_pairs={{0,2},{1,3},{2,0},{3,1},{4,6},{5,7},{6,4},{7,5},{8,10},{9,11},{10,... | collective-permute-start | bytes 12296 | tf_op jit(solution)/shard_map/ppermute | solution.py:621
  46.8 205.9 %collective-permute-start = (s32[8,128]{1,0:T(8,128)S(1)}, s32[8,128]{1,0:T(8,128)S(1)}, u32[]{:S(2)}, u32[]{:S(2)}) collective-permute-start(s32[8,128]{1,0:T(8,128)S(1)} %broadcast_in_dim.93), channel_id=1, source_target_pairs={{0,1},{1,2},{2,3},{3,0},{4,5},{5,6},{6,7},{7,4},{8,9},{9,10},{10,1... | collective-permute-start | bytes 12296 | tf_op jit(solution)/shard_map/ppermute | solution.py:621
  52.4 201.4 %copy-start.4 = (s32[6,2]{0,1:T(2,128)S(1)}, s32[6,2]{0,1:T(2,128)}, u32[]{:S(2)}) copy-start(s32[6,2]{0,1:T(2,128)} %param.30) | copy-start | bytes 148
  253.8 1.4 copy-start.2
  253.8 1.4 copy-start.3
Sparse Core Ops, SparseCore 0:
  11.2 102.0 all-gather.2

commit v2 on v1

--- a/solution.py
+++ b/solution.py
@@ -34,13 +34,13 @@
     return pairs
 
 
-def greet(peers):
+def greet(peers, seq_peers=()):
     barrier = pltpu.get_barrier_semaphore()
-    for peer in peers:
+    for axis, peer in [("keys", p) for p in peers] + [("seq", p) for p in seq_peers]:
         pl.semaphore_signal(
-            barrier, inc=1, device_id={"keys": peer}, device_id_type=pl.DeviceIdType.MESH
+            barrier, inc=1, device_id={axis: peer}, device_id_type=pl.DeviceIdType.MESH
         )
-    pl.semaphore_wait(barrier, len(peers))
+    pl.semaphore_wait(barrier, len(peers) + len(seq_peers))
 
 
 def peer_groups():
@@ -51,13 +51,13 @@
     return core, depth, row
 
 
-def send(src, dst, send_sem, recv_sem, peer):
+def send(src, dst, send_sem, recv_sem, peer, axis="keys"):
     copy = pltpu.make_async_remote_copy(
         src_ref=src,
         dst_ref=dst,
         send_sem=send_sem,
         recv_sem=recv_sem,
-        device_id={"keys": peer},
+        device_id={axis: peer},
         device_id_type=pl.DeviceIdType.MESH,
     )
     copy.start()
@@ -88,7 +88,7 @@
 
 
 def gather_ids(ids):
-    tile = jnp.zeros((8, 128), jnp.int32).at[0, : ids.size].set(ids.reshape(-1))
+    tile = jnp.pad(ids.reshape(1, -1), ((0, 7), (0, 128 - ids.size)))
     shape = (RING_Y, RING_Z, CORES, 8, 128)
     held = pl.pallas_call(
         gather_ids_kernel,
@@ -103,7 +103,7 @@
         compiler_params=pltpu.CompilerParams(collective_id=0, has_side_effects=True),
         name="gather_ids",
     )(tile)
-    return held[..., 0, : ids.size].reshape(-1)
+    return held[..., 0, : ids.size].reshape(1, -1)
 
 
 def merge(a, b):
@@ -182,6 +182,7 @@
     w_own,
     w_all,
     slab,
+    asked,
     q_ref,
     o_ref,
     best_ref,
@@ -192,11 +193,9 @@
     values,
     w_other,
     other_slab,
-    asked,
     found,
     after_depth,
     landed,
-    asked_sem,
     send_sem,
     recv_sem,
 ):
@@ -206,8 +205,8 @@
     spans = requests // 2
     near = 2 * part * parts
     rows = q_ref.shape[0] // spans
-    pairs = w_own.shape[0]
-    steps = w_all.shape[0] // pairs
+    pairs = w_own.shape[1]
+    steps = w_all.shape[1] // pairs
     core, depth, row = peer_groups()
     contract = (((1,), (1,)), ((), ()))
     dot = functools.partial(lax.dot_general, preferred_element_type=jnp.float32)
@@ -224,10 +223,9 @@
 
     def weights_flight(b):
         at = pl.ds(b * pairs, pairs)
-        return flight(w_all.at[at, pl.ds(0, 64)], w_other.at[at], SWAP + b, core[0])
+        return flight(w_all.at[:, at], w_other.at[:, at], SWAP + b, core[0])
 
     slab_flight = lambda: flight(slab, other_slab, SLAB, core[0])
-    asked_copy = lambda: pltpu.make_async_copy(w_all.at[:, pl.ds(64, 16)], asked, asked_sem)
     depth_flights = lambda: [
         flight(found, landed.at[i], DEPTH + i, peer) for i, peer in enumerate(depth)
     ]
@@ -241,7 +239,6 @@
         for b in range(steps):
             weights_flight(b).start()
         slab_flight().start()
-        asked_copy().start()
         for u in range(spans):
             for i in range(parts):
                 at = (u * parts + i) * 2 * part
@@ -250,10 +247,11 @@
     weights_flight(g).wait_recv()
     for kind, w in enumerate((wk, wv)):
         for j in range(pairs):
-            mine = pl.multiple_of(j * 64 + c * 32, 32)
-            theirs = pl.multiple_of(j * 64 + (1 - c) * 32, 32)
-            w[pl.ds(mine, 32), :] = w_own[j, kind * 32 : kind * 32 + 32, :]
-            w[pl.ds(theirs, 32), :] = w_other[g * pairs + j, kind * 32 : kind * 32 + 32, :]
+            for h in range(2):
+                mine = pl.multiple_of(j * 64 + c * 32 + h * PART, PART)
+                theirs = pl.multiple_of(j * 64 + (1 - c) * 32 + h * PART, PART)
+                w[pl.ds(mine, PART), :] = w_own[kind * 2 + h, j]
+                w[pl.ds(theirs, PART), :] = w_other[kind * 2 + h, g * pairs + j]
     keys[...] = dot(x[...], wk[...], contract).astype(jnp.bfloat16)
     values[...] = dot(x[...], wv[...], contract).astype(jnp.bfloat16)
     zero = jnp.zeros((rows, HEAD_DIM), jnp.bfloat16)
@@ -289,8 +287,7 @@
     @pl.when(g == 1)
     def _():
         slab_flight().wait_recv()
-        asked_copy().wait()
-        queries = asked[:, :, : slab.shape[1]].reshape(found.shape[1], slab.shape[1])
+        queries = asked[:, c].reshape(found.shape[1], slab.shape[1])
         found[...] = merge(
             top_two(dot(slab[...], queries, contract)), top_two(dot(other_slab[...], queries, contract))
         )
@@ -325,14 +322,14 @@
             copy.wait_send()
 
 
-def attend(pieces, w_own, slab, queries):
+def attend(pieces, w_own, slab, asked, queries):
     parts, requests, part, width = pieces.shape
     near = requests * parts * part
     tokens, columns = queries.shape
     steps = 8
-    pairs = w_own.shape[0] // steps
+    pairs = w_own.shape[1] // steps
     cols = columns // steps
-    asked = w_own.shape[0] * 16
+    found = asked.shape[0] * asked.shape[2]
     block = pl.BlockSpec((tokens, cols), lambda g: (0, g))
     flops = 2 * near * width * 2 * columns
     bf16 = jnp.bfloat16
@@ -341,29 +338,28 @@
         grid=(steps,),
         out_shape=[
             jax.ShapeDtypeStruct((tokens, columns), bf16),
-            jax.ShapeDtypeStruct((8, asked), jnp.float32),
+            jax.ShapeDtypeStruct((8, found), jnp.float32),
         ],
         in_specs=[
             pl.BlockSpec(pieces.shape, lambda g: (0, 0, 0, 0)),
-            pl.BlockSpec((pairs, w_own.shape[1], width), lambda g: (g, 0, 0)),
+            pl.BlockSpec((w_own.shape[0], pairs, part, width), lambda g: (0, g, 0, 0)),
             pl.BlockSpec(memory_space=pl.ANY),
             pl.BlockSpec(slab.shape, lambda g: (0, 0)),
+            pl.BlockSpec(asked.shape, lambda g: (0, 0, 0, 0)),
             block,
         ],
-        out_specs=[block, pl.BlockSpec((8, asked), lambda g: (0, 0))],
+        out_specs=[block, pl.BlockSpec((8, found), lambda g: (0, 0))],
         scratch_shapes=[
             pltpu.VMEM((near, width), bf16),
             pltpu.VMEM((cols, width), bf16),
             pltpu.VMEM((cols, width), bf16),
             pltpu.VMEM((near, cols), bf16),
             pltpu.VMEM((near, cols), bf16),
-            pltpu.VMEM((w_own.shape[0], 64, width), bf16),
+            pltpu.VMEM(w_own.shape, bf16),
             pltpu.VMEM(slab.shape, bf16),
-            pltpu.VMEM((w_own.shape[0], 16, width), bf16),
-            pltpu.VMEM((8, asked), jnp.float32),
-            pltpu.VMEM((8, asked), jnp.float32),
-            pltpu.VMEM((10, 8, asked), jnp.float32),
-            pltpu.SemaphoreType.DMA,
+            pltpu.VMEM((8, found), jnp.float32),
+            pltpu.VMEM((8, found), jnp.float32),
+            pltpu.VMEM((10, 8, found), jnp.float32),
             pltpu.SemaphoreType.DMA((19,)),
             pltpu.SemaphoreType.DMA((19,)),
         ],
@@ -374,63 +370,105 @@
             flops=flops, bytes_accessed=20 << 20, transcendentals=tokens * HEADS * 256
         ),
         name="attend",
-    )(pieces, w_own, w_own, slab, queries)
-
-
-def routes(all_ids):
-    requests = all_ids.shape[0]
+    )(pieces, w_own, w_own, slab, asked, queries)
+
+
+def routes_kernel(ids_ref, table_ref, before):
+    requests = ids_ref.shape[1]
     per_device = requests // (RING_Y * RING_Z * CORES)
-    index = np.arange(requests)
-    k, n = index // per_device, index % per_device
-    to_y, to_z = k // (RING_Z * CORES), (k // CORES) % RING_Z
-    tie_y = jnp.asarray((n // 2 + k) % 2 == 1)
-    tie_z = jnp.asarray((n + k) % 2 == 1)
-    order = jnp.asarray(index, jnp.int32)
-    to_y, to_z = jnp.asarray(to_y, jnp.int32), jnp.asarray(to_z, jnp.int32)
     y, z, c = place()
-    shard, offset = all_ids // 64, all_ids % 64
-    from_y, from_z, from_c = shard // (RING_Z * CORES), (shard // CORES) % RING_Z, shard % CORES
+    before[...] = jnp.where(
+        lax.broadcasted_iota(jnp.int32, before.shape, 0)
+        < lax.broadcasted_iota(jnp.int32, before.shape, 1),
+        1.0,
+        0.0,
+    ).astype(jnp.bfloat16)
+    index = lax.broadcasted_iota(jnp.int32, (1, requests), 1)
+    k = sum(jnp.where(index >= t * per_device, 1, 0) for t in range(1, requests // per_device))
+    n = index - k * per_device
+    to_y, to_z = k >> 4, (k >> 1) & 7
+    tie_y, tie_z = ((n >> 1) + k) & 1, (n + k) & 1
+    ids = ids_ref[...]
+    shard, offset = ids >> 6, ids & 63
+    from_y, from_z, from_c = shard >> 4, (shard >> 1) & 7, shard & 1
     loc = jnp.where(from_c == c, 0, 64) + offset
+    nodes = RING_Y * RING_Z * 2
+    node_rows = lax.broadcasted_iota(jnp.int32, (nodes, requests), 0)
+    lanes = lax.broadcasted_iota(jnp.int32, table_ref.shape, 1)
+    slots = lax.broadcasted_iota(jnp.int32, (table_ref.shape[0], requests), 0)
+    table = jnp.zeros(table_ref.shape, jnp.float32)
+    here = y * RING_Z + z
+
+    def column(hits, values):
+        return jnp.sum(jnp.where(hits, values.astype(jnp.float32), 0.0), axis=1, keepdims=True)
+
     base = 128
-    sends = []
-
-    def travel(position, target, ring, tie, node_of, mine, caps, loc, base):
-        ahead = (target - position) % ring
-        back = (ahead > ring // 2) | ((ahead == ring // 2) & tie)
-        left = jnp.where(back, (ring - ahead) % ring, ahead)
+    r = 0
+    stuck = jnp.zeros((1, requests), jnp.int32)
+    for along_y, caps in ((True, Y_CAPS), (False, Z_CAPS)):
+        ring = RING_Y if along_y else RING_Z
+        position, target, tie = (from_y, to_y, tie_y) if along_y else (from_z, to_z, tie_z)
+        ahead = (target - position) & (ring - 1)
+        back = (ahead > ring // 2) | ((ahead == ring // 2) & (tie == 1))
+        left = jnp.where(back, (ring - ahead) & (ring - 1), ahead)
         step = jnp.where(back, ring - 1, 1)
-        way = back.astype(jnp.int32)
+        way = jnp.where(back, 1, 0)
         for width in caps:
-            node = node_of(position) * 2 + way
-            moving = left > 0
-            seat = jnp.where(moving, node, -1)
-            priority = (16 - left) * 1024 + order
-            before = (seat[:, None] == seat[None, :]) & (priority[:, None] < priority[None, :])
-            rank = jnp.sum(before.astype(jnp.int32), axis=0)
-            goes = moving & (rank < width)
-            seat_rank = jnp.where(goes, node * 64 + rank, -1)
-            wanted = (mine * 2 + np.arange(2, dtype=np.int32))[:, None] * 64 + np.arange(
-                width, dtype=np.int32
+            chip = position * RING_Z + from_z if along_y else to_y * RING_Z + position
+            node = chip * 2 + way
+            seat = node_rows == node
+            kinds = [
+                jnp.where(seat & (left == d), 1.0, 0.0) for d in range(ring // 2, 0, -1)
+            ]
+            counts = lax.dot_general(
+                jnp.concatenate(kinds, axis=0).astype(jnp.bfloat16),
+                before[...],
+                (((1,), (0,)), ((), ())),
+                preferred_element_type=jnp.float32,
             )
-            hit = seat_rank[None, None, :] == wanted[:, :, None]
-            sends.append(jnp.sum(jnp.where(hit, loc[None, None, :], 0), axis=-1))
+            rank = jnp.zeros((1, requests), jnp.float32)
+            ahead_of = jnp.zeros((nodes, 1), jnp.float32)
+            for i, kind in enumerate(kinds):
+                mine = counts[i * nodes : (i + 1) * nodes] + ahead_of
+                rank += jnp.sum(kind * mine, axis=0, keepdims=True)
+                ahead_of += jnp.sum(kind, axis=1, keepdims=True)
+            rank = rank.astype(jnp.int32)
+            goes = (left > 0) & (rank < width)
+            slot = jnp.where(goes & (chip == here), way * width + rank, -1)
+            table = jnp.where(lanes == r, column(slots == slot, loc), table)
             loc = jnp.where(goes, base + way * width + rank, loc)
             base += 2 * width
-            position = jnp.where(goes, (position + step) % ring, position)
-            left = left - goes.astype(jnp.int32)
-        return jnp.max(left), loc, base
-
-    stuck_y, loc, base = travel(
-        from_y, to_y, RING_Y, tie_y, lambda p: p * RING_Z + from_z, y * RING_Z + z, Y_CAPS, loc, base
-    )
-    stuck_z, loc, base = travel(
-        from_z, to_z, RING_Z, tie_z, lambda p: to_y * RING_Z + p, y * RING_Z + z, Z_CAPS, loc, base
-    )
-    table = loc.reshape(RING_Y * RING_Z, CORES, per_device)
-    here = lax.dynamic_index_in_dim(table, y * RING_Z + z, 0, False)
-    own = lax.dynamic_index_in_dim(here, c, 0, False)
-    other = lax.dynamic_index_in_dim(here, 1 - c, 0, False)
-    return sends, jnp.stack([own, other]), jnp.maximum(stuck_y, stuck_z)
+            position = jnp.where(goes, (position + step) & (ring - 1), position)
+            left = left - jnp.where(goes, 1, 0)
+            r += 1
+        stuck = jnp.maximum(stuck, left)
+    for core in (c, 1 - c):
+        first = (here * CORES + core) * per_device
+        wanted = (index == first + slots) & (slots < per_device)
+        table = jnp.where(lanes == r, column(wanted, loc), table)
+        r += 1
+    worst = jnp.max(stuck.astype(jnp.float32), axis=1, keepdims=True)
+    table = jnp.where(lanes == r, worst, table)
+    table_ref[...] = table.astype(jnp.int32)
+
+
+def routes(all_ids):
+    requests = all_ids.shape[1]
+    return pl.pallas_call(
+        routes_kernel,
+        out_shape=jax.ShapeDtypeStruct((2 * max(WIDTHS), 128), jnp.int32),
+        in_specs=[pl.BlockSpec(memory_space=pltpu.VMEM)],
+        out_specs=pl.BlockSpec(memory_space=pltpu.VMEM),
+        scratch_shapes=[pltpu.VMEM((requests, requests), jnp.bfloat16)],
+        name="routes",
+    )(all_ids)
+
+
+MOVES = [(1, 0)] * len(Y_CAPS) + [(0, 1)] * len(Z_CAPS)
+WIDTHS = Y_CAPS + Z_CAPS
+CHUNKS = 4
+REQUESTS = 12
+PART = 16
 
 
 def issue_order(moves, widths, chunks):
@@ -455,25 +493,49 @@
     return order
 
 
-MOVES = [(1, 0)] * len(Y_CAPS) + [(0, 1)] * len(Z_CAPS)
-WIDTHS = Y_CAPS + Z_CAPS
-CHUNKS = 4
-PART = 16
-
-
-def carry_kernel(requests, locs_ref, final_ref, store_ref, out_ref, held, *rest):
+def carry_kernel(requests, table_ref, store_ref, kv_ref, out_ref, w_ref, held, *rest):
     rounds = len(MOVES)
     total = CHUNKS * rounds
     out_bufs = rest[:total]
     in_bufs = rest[total : 2 * total]
-    last, swap_sems, send_sems, recv_sems = rest[2 * total :]
+    last, swap_sems, send_sems, recv_sems, w_send_sems, w_recv_sems = rest[2 * total :]
     y, z, c = place()
     half = held.shape[1]
     spans = store_ref.shape[0]
     steps = [((y + dy) % RING_Y, (z + dz) % RING_Z) for dy, dz in ((1, 0), (-1, 0), (0, 1), (0, -1))]
     near = [key_of(a + 0, b + 0, c) for a, b in steps]
     buddy = key_of(y, z, 1 - c)
-    greet(near + [buddy])
+    _, depth, row = peer_groups()
+    x, planes = lax.axis_index("seq"), lax.axis_size("seq")
+    seq = [lax.rem(x + d, planes) for d in range(1, planes)]
+    greet(depth + row + [buddy], seq)
+    quarter = kv_ref.at[x // 2, pl.ds(pl.multiple_of((x % 2) * PART, PART), PART)]
+    pair = y * RING_Z + z
+    own = pltpu.make_async_copy(quarter, w_ref.at[x, pair], swap_sems.at[3])
+    own.start()
+    w_flights = [
+        [
+            send(quarter, w_ref.at[x, pair], w_send_sems.at[i], w_recv_sems.at[i], peer)
+            for i, peer in enumerate(depth)
+        ]
+    ]
+
+    def pass_on(stage):
+        if stage == 1:
+            own.wait()
+        for copy in w_flights[-1]:
+            copy.wait_recv()
+        if stage == 1:
+            part, peers, at, axis = w_ref.at[x, pl.ds(y * RING_Z, RING_Z)], row, 7, "keys"
+        else:
+            part, peers, at, axis = w_ref.at[x], seq, 10, "seq"
+        w_flights.append(
+            [
+                send(part, part, w_send_sems.at[at + i], w_recv_sems.at[at + i], peer, axis)
+                for i, peer in enumerate(peers)
+            ]
+        )
+
     mine = pl.ds(pl.multiple_of(c * half, half), half)
     theirs = pl.ds(pl.multiple_of((1 - c) * half, half), half)
     swap = send(
@@ -509,7 +571,7 @@
         buf = out_bufs[j * rounds + r]
 
         def fill(s, carry):
-            buf[s] = picked(j, r, locs_ref[r, s])
+            buf[s] = picked(j, r, table_ref[s, r])
             return carry
 
         lax.fori_loop(0, 2 * width, fill, 0)
@@ -526,8 +588,8 @@
         land(j, rounds - 1)
 
         def fill(s, carry):
-            out_ref[2 * j, s] = picked(j, rounds, final_ref[0, s])
-            last[j, s] = picked(j, rounds, final_ref[1, s])
+            out_ref[2 * j, s] = picked(j, rounds, table_ref[s, rounds])
+            last[j, s] = picked(j, rounds, table_ref[s, rounds + 1])
             return carry
 
         lax.fori_loop(0, requests, fill, 0)
@@ -543,42 +605,49 @@
             waiting.append(j)
         elif waiting:
             finish(waiting.pop(0))
+        if (j, r) in ((1, 1), (2, 1)):
+            pass_on(j)
     for j in waiting:
         finish(j)
     for j in range(CHUNKS):
         land(j, rounds)
-    for copies in flights.values():
+    for copy in w_flights[-1]:
+        copy.wait_recv()
+    for copies in list(flights.values()) + w_flights:
         for copy in copies:
             copy.wait_send()
 
 
-def carry(store, sends, final):
+def carry(store, kv_weight, table):
     spans, rows, enc_width = store.shape
-    requests = final.shape[1]
-    longest = 2 * max(WIDTHS)
-    locs = jnp.stack([jnp.pad(t.reshape(-1), (0, longest - t.size)) for t in sends])
+    planes = lax.axis_size("seq")
     item = (PART, enc_width)
     bufs = [pltpu.VMEM((2 * w, *item), store.dtype) for _ in range(CHUNKS) for w in WIDTHS]
     copies = 2 * len(bufs) + CHUNKS
     return pl.pallas_call(
-        functools.partial(carry_kernel, requests),
-        out_shape=jax.ShapeDtypeStruct((2 * CHUNKS, requests, *item), store.dtype),
-        in_specs=[pl.BlockSpec(memory_space=pltpu.SMEM)] * 2 + [pl.BlockSpec(memory_space=pl.ANY)],
-        out_specs=pl.BlockSpec(memory_space=pltpu.VMEM),
+        functools.partial(carry_kernel, REQUESTS),
+        out_shape=[
+            jax.ShapeDtypeStruct((2 * CHUNKS, REQUESTS, *item), store.dtype),
+            jax.ShapeDtypeStruct((planes, RING_Y * RING_Z, *item), store.dtype),
+        ],
+        in_specs=[pl.BlockSpec(memory_space=pltpu.SMEM)] + [pl.BlockSpec(memory_space=pl.ANY)] * 2,
+        out_specs=[pl.BlockSpec(memory_space=pltpu.VMEM)] * 2,
         scratch_shapes=[pltpu.VMEM((2 * spans, rows // 2, enc_width), store.dtype)]
         + bufs * 2
         + [
-            pltpu.VMEM((CHUNKS, requests, *item), store.dtype),
-            pltpu.SemaphoreType.DMA((3,)),
+            pltpu.VMEM((CHUNKS, REQUESTS, *item), store.dtype),
+            pltpu.SemaphoreType.DMA((4,)),
             pltpu.SemaphoreType.DMA((copies,)),
             pltpu.SemaphoreType.DMA((copies,)),
+            pltpu.SemaphoreType.DMA((13,)),
+            pltpu.SemaphoreType.DMA((13,)),
         ],
         compiler_params=pltpu.CompilerParams(
             collective_id=2, has_side_effects=True, vmem_limit_bytes=60 << 20
         ),
         cost_estimate=pl.CostEstimate(flops=0, bytes_accessed=500 << 20, transcendentals=0),
         name="carry",
-    )(locs, final, store)
+    )(table, store, kv_weight)
 
 
 def direct(neighbour_store, neighbour_ids):
@@ -605,22 +674,19 @@
     y, z, c = place()
     own_spans = neighbour_ids.shape[0]
     span_rows = neighbour_store.shape[1]
-    enc_width = neighbour_store.shape[2]
     all_ids = gather_ids(neighbour_ids)
-    asked = jnp.zeros((16, enc_width), span_queries.dtype)
-    asked = lax.dynamic_update_slice(asked, span_queries, (0, 0))
-    shard = jnp.concatenate([kv_weight[0], kv_weight[1], asked], axis=0)
-    groups = [[key_of(a, b, d) for a in range(RING_Y) for b in range(RING_Z)] for d in range(CORES)]
-    weight_own = lax.all_gather(shard, "keys", axis=0, axis_index_groups=groups)
-    sends, final, stuck = routes(all_ids)
-    flag = jnp.full((8, 128), stuck, jnp.int32)
+    asked = jnp.pad(span_queries, ((0, 16 - own_spans), (0, 0)))
+    all_asked = lax.all_gather(asked, "keys", axis=0, tiled=True)
+    all_asked = all_asked.reshape(RING_Y * RING_Z, CORES, *asked.shape)
+    table = routes(all_ids)
+    flag = table[:8]
     seq = lax.axis_size("seq")
     worst = flag
     for d in range(1, seq):
         worst = jnp.maximum(
             worst, lax.ppermute(flag, "seq", [(s, (s + d) % seq) for s in range(seq)])
         )
-    pieces = carry(neighbour_store, sends, final)
+    pieces, weight_own = carry(neighbour_store, kv_weight, table)
 
     def resend(store, ids, fast):
         return jnp.stack(
@@ -632,9 +698,9 @@
         )
 
     pieces = lax.cond(
-        worst[0, 0] > 0, resend, lambda store, ids, fast: fast, neighbour_store, neighbour_ids, pieces
+        worst[0, len(WIDTHS) + 2] > 0, resend, lambda store, ids, fast: fast, neighbour_store, neighbour_ids, pieces
     )
-    attended, best = attend(pieces, weight_own, key_slab, attn_queries)
+    attended, best = attend(pieces, weight_own, key_slab, all_asked, attn_queries)
     column = (position // CORES) * 16
     best_scores = lax.dynamic_slice_in_dim(best, column, own_spans, axis=1)[:2].T
     return (best_scores, attended)

time: 294 us -> 284 us (0.966)
  other arithmetic: 14.6 us -> 0.7 us
  Pallas kernels: 250 us -> 254 us
    select_n x9 -> x0, other arithmetic: 7.31 us -> none  [the longest x4 2.98 us: travel(): seat = jnp.where(moving, node, -1)]
    pallas_call x1 -> x2, Pallas kernels: 200 us -> 205 us  [the longest x1 201 us: carry(): pl.pallas_call(functools.partial(carry_kernel, REQUESTS), out_shape=[jax....]
    reduce_sum x11 -> x0, other arithmetic: 4.62 us -> none  [the longest x6 2.73 us: travel(): rank = jnp.sum(before.astype(jnp.int32), axis=0)]
  transfers between devices with their start and end apart: 4 -> 4, of which waited for: 0 -> 0; matrix products, arithmetic and copies ran while one was open for 6% -> 2% of each run, Pallas kernels for 75% -> 80%
where the time goes in v2:
time: 284 us; the launch traced here: 283 us
  Pallas kernels  254 us (89%)
  between operations  14.8 us (5%)
  local copies, waits for them, and re-layouts  10.2 us (4%)
  starting transfers between devices  3.64 us (1%)
    pallas_call x1, Pallas kernels, carry(): pl.pallas_call(functools.partial(carry_kernel, REQUESTS), out_shape=[jax....  201 us
    pallas_call x1, Pallas kernels, attend(): pl.pallas_call(attend_kernel, grid=(steps,), out_shape=[jax.ShapeDtypeStr...  28.5 us
    pallas_call x1, Pallas kernels, gather_ids(): pl.pallas_call(gather_ids_kernel, out_shape=jax.ShapeDtypeStruct(shape, j...  20.2 us
  transfers between devices with their start and end apart: 4, of which 0 were waited for; matrix products, arithmetic and copies ran while one was open for 2% of the time, Pallas kernels for 80%

profile of v2, /device:TPU:1, one launch (start us, length us, event | category | flops | bytes accessed | tf_op | source)
XLA Modules:
  0.0 283.3 jit_solution(2787931772486479209)
XLA Ops:
  7.2 0.0 all-gather.2.cloned.1.call-start
  7.2 1.3 pad.9
  8.5 0.0 all-gather.2.cloned.1.call-update
  8.5 0.8 copy.19
  9.3 0.1 reshape.167
  9.4 0.6 pad.8.ids_ref
  10.0 20.2 %gather_ids.1 = s32[4,8,2,8,128]{4,3,2,1,0:T(8,128)} custom-call(s32[8,128]{1,0:T(8,128)} %pad.8.ids_ref), custom_call_target="tpu_custom_call" | custom-call | tf_op jit(solution)/shard_map/gather_ids/pallas_call | solution.py:93
  30.2 1.1 slice_reduce_fusion
  31.2 0.7 reshape_squeeze.3.ids_ref
  32.0 3.8 %routes.1.table_ref = s32[48,128]{1,0:T(8,128)} custom-call(s32[1,768]{1,0:T(1,128)} %reshape_squeeze.3.ids_ref), custom_call_target="tpu_custom_call" | custom-call | tf_op jit(solution)/shard_map/routes/pallas_call | solution.py:457
  35.8 0.7 slice.40
  36.5 2.5 collective-permute-start.2
  38.9 0.5 collective-permute-start.1
  39.5 0.6 collective-permute-start
  40.1 0.0 copy-start.5
  40.1 201.3 %carry.1 = (bf16[8,12,16,896]{3,2,1,0:T(8,128)(2,1)}, bf16[4,32,16,896]{3,2,1,0:T(8,128)(2,1)}) custom-call(s32[48,128]{1,0:T(8,128)} %routes.1.table_ref, bf16[64,64,896]{2,1,0:T(8,128)(2,1)} %store_ref.1, bf16[2,32,896]{2,1,0:T(8,128)(2,1)} %kv_ref.1), custom_call_target="tpu_custom_call" | custom-call | bytes 524288000 | tf_op jit(solution)/shard_map/carry/pallas_call | solution.py:627
  241.3 0.0 collective-permute-done.2
  241.4 0.0 collective-permute-done.1
  241.4 0.0 collective-permute-done
  241.4 0.7 maximum_maximum_fusion
  242.1 0.6 slice.38
  243.3 0.0 copy-done.5
  243.3 0.0 copy-start.2
  243.3 0.0 copy-start.4
  243.3 0.2 conditional.1
  243.5 0.0 all-gather.2.cloned.1.call-done
  243.6 1.2 copy-done.2
  244.7 0.0 copy-done.4
  244.7 0.0 copy-start.3
  244.7 1.4 copy-done.3
  246.1 28.5 %attend.1 = (bf16[384,2048]{1,0:T(8,128)(2,1)S(1)}, f32[8,512]{1,0:T(8,128)S(1)}) custom-call(bf16[8,12,16,896]{3,2,1,0:T(8,128)(2,1)} %get-tuple-element.42.pieces, bf16[4,32,16,896]{3,2,1,0:T(8,128)(2,1)} %get-tuple-element.21.w_own.w_all, bf16[4,32,16,896]{3,2,1,0:T(8,128)(2,1)} %get-tuple-element.21.w_own.w_all, bf16[64,768]{1,0:T(8,128)(2,1)S(1)} %copy-done.4, ...), custom_call_target="tpu_custom_call" | custom-call | flops 11274289152 | bytes 20971520 | tf_op jit(solution)/shard_map/attend/pallas_call | solution.py:336
  274.7 0.1 constant_dynamic-slice_fusion
  274.8 0.6 slice_bitcast_fusion
  275.3 1.1 copy.31
Async XLA Ops:
  7.2 236.4 %all-gather.2.cloned.1.call-start = ((), (), s32[]{:S(2)}) async-start(), calls=%async_computation.3 | async-start | bytes 1597440 | tf_op jit(solution)/shard_map/all_gather | solution.py:679
  36.5 204.9 %collective-permute-start.2 = (s32[8,128]{1,0:T(8,128)S(1)}, s32[8,128]{1,0:T(8,128)S(1)}, u32[]{:S(2)}, u32[]{:S(2)}) collective-permute-start(s32[8,128]{1,0:T(8,128)S(1)} %slice.40), channel_id=1, source_target_pairs={{0,3},{1,0},{2,1},{3,2},{4,7},{5,4},{6,5},{7,6},{8,11},{9,8},{10,9... | collective-permute-start | bytes 12296 | tf_op jit(solution)/shard_map/ppermute | solution.py:687
  38.9 202.4 %collective-permute-start.1 = (s32[8,128]{1,0:T(8,128)S(1)}, s32[8,128]{1,0:T(8,128)S(1)}, u32[]{:S(2)}, u32[]{:S(2)}) collective-permute-start(s32[8,128]{1,0:T(8,128)S(1)} %slice.40), channel_id=1, source_target_pairs={{0,2},{1,3},{2,0},{3,1},{4,6},{5,7},{6,4},{7,5},{8,10},{9,11},{10,... | collective-permute-start | bytes 12296 | tf_op jit(solution)/shard_map/ppermute | solution.py:687
  39.5 201.9 %collective-permute-start = (s32[8,128]{1,0:T(8,128)S(1)}, s32[8,128]{1,0:T(8,128)S(1)}, u32[]{:S(2)}, u32[]{:S(2)}) collective-permute-start(s32[8,128]{1,0:T(8,128)S(1)} %slice.40), channel_id=1, source_target_pairs={{0,1},{1,2},{2,3},{3,0},{4,5},{5,6},{6,7},{7,4},{8,9},{9,10},{10,1... | collective-permute-start | bytes 12296 | tf_op jit(solution)/shard_map/ppermute | solution.py:687
  40.1 203.2 %copy-start.5 = (s32[6,2]{0,1:T(2,128)S(1)}, s32[6,2]{0,1:T(2,128)}, u32[]{:S(2)}) copy-start(s32[6,2]{0,1:T(2,128)} %param.11) | copy-start | bytes 148
  243.3 1.4 copy-start.2
  243.3 1.4 copy-start.4
  244.7 1.4 copy-start.3
Sparse Core Ops, SparseCore 0:
  10.7 81.6 all-gather.1

commit v3 on v2

--- a/solution.py
+++ b/solution.py
@@ -11,8 +11,15 @@
 HEADS = 16
 HEAD_DIM = 128
 RING_Y, RING_Z, CORES = 4, 8, 2
-Y_CAPS = (24, 17)
-Z_CAPS = (12, 12, 11, 10)
+Y_CAPS, Z_CAPS = (24, 17), (12, 12, 11, 10)
+Z_FIRST_CAPS, Y_LAST_CAPS = (19, 16, 16, 15), (14, 11)
+TRIPS = (((True, Y_CAPS), (False, Z_CAPS)), ((False, Z_FIRST_CAPS), (True, Y_LAST_CAPS)))
+MOVES = tuple([along for along, caps in trip for _ in caps] for trip in TRIPS)
+WIDTHS = tuple([w for _, caps in trip for w in caps] for trip in TRIPS)
+CHUNK_TRIPS = (0, 0, 0, 1)
+COLUMNS = 8
+PART = 16
+REQUESTS = 12
 
 
 def key_of(y, z, c):
@@ -402,53 +409,58 @@
     def column(hits, values):
         return jnp.sum(jnp.where(hits, values.astype(jnp.float32), 0.0), axis=1, keepdims=True)
 
-    base = 128
-    r = 0
     stuck = jnp.zeros((1, requests), jnp.int32)
-    for along_y, caps in ((True, Y_CAPS), (False, Z_CAPS)):
-        ring = RING_Y if along_y else RING_Z
-        position, target, tie = (from_y, to_y, tie_y) if along_y else (from_z, to_z, tie_z)
-        ahead = (target - position) & (ring - 1)
-        back = (ahead > ring // 2) | ((ahead == ring // 2) & (tie == 1))
-        left = jnp.where(back, (ring - ahead) & (ring - 1), ahead)
-        step = jnp.where(back, ring - 1, 1)
-        way = jnp.where(back, 1, 0)
-        for width in caps:
-            chip = position * RING_Z + from_z if along_y else to_y * RING_Z + position
-            node = chip * 2 + way
-            seat = node_rows == node
-            kinds = [
-                jnp.where(seat & (left == d), 1.0, 0.0) for d in range(ring // 2, 0, -1)
-            ]
-            counts = lax.dot_general(
-                jnp.concatenate(kinds, axis=0).astype(jnp.bfloat16),
-                before[...],
-                (((1,), (0,)), ((), ())),
-                preferred_element_type=jnp.float32,
-            )
-            rank = jnp.zeros((1, requests), jnp.float32)
-            ahead_of = jnp.zeros((nodes, 1), jnp.float32)
-            for i, kind in enumerate(kinds):
-                mine = counts[i * nodes : (i + 1) * nodes] + ahead_of
-                rank += jnp.sum(kind * mine, axis=0, keepdims=True)
-                ahead_of += jnp.sum(kind, axis=1, keepdims=True)
-            rank = rank.astype(jnp.int32)
-            goes = (left > 0) & (rank < width)
-            slot = jnp.where(goes & (chip == here), way * width + rank, -1)
-            table = jnp.where(lanes == r, column(slots == slot, loc), table)
-            loc = jnp.where(goes, base + way * width + rank, loc)
-            base += 2 * width
-            position = jnp.where(goes, (position + step) & (ring - 1), position)
-            left = left - jnp.where(goes, 1, 0)
+    first_loc = loc
+    for t, trip in enumerate(TRIPS):
+        base, r, loc = 128, t * COLUMNS, first_loc
+        for leg, (along_y, caps) in enumerate(trip):
+            ring = RING_Y if along_y else RING_Z
+            position, target, tie = (from_y, to_y, tie_y) if along_y else (from_z, to_z, tie_z)
+            if along_y:
+                other = to_z if leg else from_z
+            else:
+                other = to_y if leg else from_y
+            ahead = (target - position) & (ring - 1)
+            back = (ahead > ring // 2) | ((ahead == ring // 2) & (tie == 1))
+            left = jnp.where(back, (ring - ahead) & (ring - 1), ahead)
+            step = jnp.where(back, ring - 1, 1)
+            way = jnp.where(back, 1, 0)
+            for width in caps:
+                chip = position * RING_Z + other if along_y else other * RING_Z + position
+                node = chip * 2 + way
+                seat = node_rows == node
+                kinds = [
+                    jnp.where(seat & (left == d), 1.0, 0.0) for d in range(ring // 2, 0, -1)
+                ]
+                counts = lax.dot_general(
+                    jnp.concatenate(kinds, axis=0).astype(jnp.bfloat16),
+                    before[...],
+                    (((1,), (0,)), ((), ())),
+                    preferred_element_type=jnp.float32,
+                )
+                rank = jnp.zeros((1, requests), jnp.float32)
+                ahead_of = jnp.zeros((nodes, 1), jnp.float32)
+                for i, kind in enumerate(kinds):
+                    mine = counts[i * nodes : (i + 1) * nodes] + ahead_of
+                    rank += jnp.sum(kind * mine, axis=0, keepdims=True)
+                    ahead_of += jnp.sum(kind, axis=1, keepdims=True)
+                rank = rank.astype(jnp.int32)
+                goes = (left > 0) & (rank < width)
+                slot = jnp.where(goes & (chip == here), way * width + rank, -1)
+                table = jnp.where(lanes == r, column(slots == slot, loc), table)
+                loc = jnp.where(goes, base + way * width + rank, loc)
+                base += 2 * width
+                position = jnp.where(goes, (position + step) & (ring - 1), position)
+                left = left - jnp.where(goes, 1, 0)
+                r += 1
+            stuck = jnp.maximum(stuck, left)
+        for core in (c, 1 - c):
+            first = (here * CORES + core) * per_device
+            wanted = (index == first + slots) & (slots < per_device)
+            table = jnp.where(lanes == r, column(wanted, loc), table)
             r += 1
-        stuck = jnp.maximum(stuck, left)
-    for core in (c, 1 - c):
-        first = (here * CORES + core) * per_device
-        wanted = (index == first + slots) & (slots < per_device)
-        table = jnp.where(lanes == r, column(wanted, loc), table)
-        r += 1
     worst = jnp.max(stuck.astype(jnp.float32), axis=1, keepdims=True)
-    table = jnp.where(lanes == r, worst, table)
+    table = jnp.where(lanes == len(TRIPS) * COLUMNS, worst, table)
     table_ref[...] = table.astype(jnp.int32)
 
 
@@ -456,7 +468,7 @@
     requests = all_ids.shape[1]
     return pl.pallas_call(
         routes_kernel,
-        out_shape=jax.ShapeDtypeStruct((2 * max(WIDTHS), 128), jnp.int32),
+        out_shape=jax.ShapeDtypeStruct((2 * max(WIDTHS[0] + WIDTHS[1]), 128), jnp.int32),
         in_specs=[pl.BlockSpec(memory_space=pltpu.VMEM)],
         out_specs=pl.BlockSpec(memory_space=pltpu.VMEM),
         scratch_shapes=[pltpu.VMEM((requests, requests), jnp.bfloat16)],
@@ -464,46 +476,24 @@
     )(all_ids)
 
 
-MOVES = [(1, 0)] * len(Y_CAPS) + [(0, 1)] * len(Z_CAPS)
-WIDTHS = Y_CAPS + Z_CAPS
-CHUNKS = 4
-REQUESTS = 12
-PART = 16
-
-
-def issue_order(moves, widths, chunks):
-    done = {(j, -1): 0.0 for j in range(chunks)}
-    issued, order, free, clock = set(), [], {True: 0.0, False: 0.0}, 0.0
-    while len(order) < chunks * len(moves):
-        ready = []
-        for j in range(chunks):
-            r = sum((j, q) in issued for q in range(len(moves)))
-            if r == len(moves) or (j, r - 1) not in done:
-                continue
-            if r == 0 and j >= 2 and (j - 2, len(Y_CAPS) - 1) not in issued:
-                continue
-            ready.append((max(clock, done[j, r - 1] + 2.5 * (r > 0)), j, r))
-        at, j, r = min(ready)
-        along_y = moves[r][0] != 0
-        clock = at + 0.5
-        free[along_y] = max(free[along_y], clock) + 0.65 * widths[r]
-        done[j, r] = free[along_y]
-        issued.add((j, r))
-        order.append((j, r))
-    return order
-
-
-def carry_kernel(requests, table_ref, store_ref, kv_ref, out_ref, w_ref, held, *rest):
-    rounds = len(MOVES)
-    total = CHUNKS * rounds
+ISSUES = (
+    ((3, 0), (1, 0), (0, 0), (3, 1), (1, 1), (3, 2), (0, 1), (3, 3), (2, 0), (1, 2), (0, 2), (1, 3))
+    + ((2, 1), (0, 3), (1, 4), (-1, 1), (2, 2), (3, 4), (-1, 2), (0, 4), (2, 3), (3, 5), (0, 5))
+    + ((2, 4), (1, 5), (2, 5))
+)
+
+
+def carry_kernel(table_ref, store_ref, kv_ref, out_ref, w_ref, *rest):
+    rounds = len(MOVES[0])
+    total = len(CHUNK_TRIPS) * rounds
+    held, rest = rest[:2], rest[2:]
     out_bufs = rest[:total]
     in_bufs = rest[total : 2 * total]
     last, swap_sems, send_sems, recv_sems, w_send_sems, w_recv_sems = rest[2 * total :]
     y, z, c = place()
-    half = held.shape[1]
     spans = store_ref.shape[0]
     steps = [((y + dy) % RING_Y, (z + dz) % RING_Z) for dy, dz in ((1, 0), (-1, 0), (0, 1), (0, -1))]
-    near = [key_of(a + 0, b + 0, c) for a, b in steps]
+    near = [key_of(a, b, c) for a, b in steps]
     buddy = key_of(y, z, 1 - c)
     _, depth, row = peer_groups()
     x, planes = lax.axis_index("seq"), lax.axis_size("seq")
@@ -511,7 +501,7 @@
     greet(depth + row + [buddy], seq)
     quarter = kv_ref.at[x // 2, pl.ds(pl.multiple_of((x % 2) * PART, PART), PART)]
     pair = y * RING_Z + z
-    own = pltpu.make_async_copy(quarter, w_ref.at[x, pair], swap_sems.at[3])
+    own = pltpu.make_async_copy(quarter, w_ref.at[x, pair], swap_sems.at[6])
     own.start()
     w_flights = [
         [
@@ -536,26 +526,35 @@
             ]
         )
 
-    mine = pl.ds(pl.multiple_of(c * half, half), half)
-    theirs = pl.ds(pl.multiple_of((1 - c) * half, half), half)
-    swap = send(
-        store_ref.at[:, theirs], held.at[pl.ds(spans, spans)], swap_sems.at[0], swap_sems.at[1], buddy
-    )
-    keep = pltpu.make_async_copy(store_ref.at[:, mine], held.at[pl.ds(0, spans)], swap_sems.at[2])
-    keep.start()
-    swap.wait()
-    keep.wait()
-    bases = np.concatenate([[2 * spans], 2 * spans + np.cumsum(2 * np.array(WIDTHS))]).tolist()
+    halves = {}
+    for part in (1, 0):
+        mine = pl.ds(pl.multiple_of((2 * c + part) * PART, PART), PART)
+        theirs = pl.ds(pl.multiple_of((2 * (1 - c) + part) * PART, PART), PART)
+        keep = pltpu.make_async_copy(
+            store_ref.at[:, mine], held[part].at[pl.ds(0, spans)], swap_sems.at[3 * part + 2]
+        )
+        keep.start()
+        swap = send(
+            store_ref.at[:, theirs],
+            held[part].at[pl.ds(spans, spans)],
+            swap_sems.at[3 * part],
+            swap_sems.at[3 * part + 1],
+            buddy,
+        )
+        halves[part] = (swap, keep)
+    ready = set()
+    bases = [
+        np.concatenate([[2 * spans], 2 * spans + np.cumsum(2 * np.array(w))]).tolist() for w in WIDTHS
+    ]
 
     def picked(j, r, at):
         step, part = j // 2, j % 2
-        rows = slice(part * PART, (part + 1) * PART)
-        here = jnp.where(at < 2 * spans, at + step, 0)
-        value = held[here, rows, :]
+        value = held[part][jnp.where(at < 2 * spans, at + step, 0)]
         for q in range(r):
-            count = 2 * WIDTHS[q]
-            inside = (at >= bases[q]) & (at < bases[q] + count)
-            value = jnp.where(inside, in_bufs[j * rounds + q][jnp.where(inside, at - bases[q], 0)], value)
+            base, count = bases[CHUNK_TRIPS[j]][q], 2 * WIDTHS[CHUNK_TRIPS[j]][q]
+            inside = (at >= base) & (at < base + count)
+            block = in_bufs[j * rounds + q][jnp.where(inside, at - base, 0)]
+            value = jnp.where(inside, block, value)
         return value
 
     flights = {}
@@ -565,13 +564,18 @@
             flight.wait_recv()
 
     def issue(j, r):
+        trip = CHUNK_TRIPS[j]
         if r > 0:
             land(j, r - 1)
-        width = WIDTHS[r]
+        elif j % 2 not in ready:
+            ready.add(j % 2)
+            for copy in halves[j % 2]:
+                copy.wait()
+        width = WIDTHS[trip][r]
         buf = out_bufs[j * rounds + r]
 
         def fill(s, carry):
-            buf[s] = picked(j, r, table_ref[s, r])
+            buf[s] = picked(j, r, table_ref[s, trip * COLUMNS + r])
             return carry
 
         lax.fori_loop(0, 2 * width, fill, 0)
@@ -579,37 +583,39 @@
         for d in range(2):
             part = pl.ds(d * width, width)
             k = (j * rounds + r) * 2 + d
-            peer = near[d if MOVES[r][0] else 2 + d]
+            peer = near[d if MOVES[trip][r] else 2 + d]
             flights[j, r].append(
                 send(buf.at[part], in_bufs[j * rounds + r].at[part], send_sems.at[k], recv_sems.at[k], peer)
             )
 
     def finish(j):
         land(j, rounds - 1)
+        column = CHUNK_TRIPS[j] * COLUMNS + rounds
 
         def fill(s, carry):
-            out_ref[2 * j, s] = picked(j, rounds, table_ref[s, rounds])
-            last[j, s] = picked(j, rounds, table_ref[s, rounds + 1])
+            out_ref[2 * j, s] = picked(j, rounds, table_ref[s, column])
+            last[j, s] = picked(j, rounds, table_ref[s, column + 1])
             return carry
 
-        lax.fori_loop(0, requests, fill, 0)
+        lax.fori_loop(0, REQUESTS, fill, 0)
         k = 2 * total + j
         flights[j, rounds] = [
             send(last.at[j], out_ref.at[2 * j + 1], send_sems.at[k], recv_sems.at[k], buddy)
         ]
 
     waiting = []
-    for j, r in issue_order(MOVES, WIDTHS, CHUNKS):
+    for j, r in ISSUES:
+        if j < 0:
+            pass_on(r)
+            continue
         issue(j, r)
         if r == rounds - 1:
             waiting.append(j)
         elif waiting:
             finish(waiting.pop(0))
-        if (j, r) in ((1, 1), (2, 1)):
-            pass_on(j)
     for j in waiting:
         finish(j)
-    for j in range(CHUNKS):
+    for j in range(len(CHUNK_TRIPS)):
         land(j, rounds)
     for copy in w_flights[-1]:
         copy.wait_recv()
@@ -619,24 +625,25 @@
 
 
 def carry(store, kv_weight, table):
-    spans, rows, enc_width = store.shape
+    spans, _, enc_width = store.shape
     planes = lax.axis_size("seq")
     item = (PART, enc_width)
-    bufs = [pltpu.VMEM((2 * w, *item), store.dtype) for _ in range(CHUNKS) for w in WIDTHS]
-    copies = 2 * len(bufs) + CHUNKS
+    chunks = len(CHUNK_TRIPS)
+    bufs = [pltpu.VMEM((2 * w, *item), store.dtype) for t in CHUNK_TRIPS for w in WIDTHS[t]]
+    copies = 2 * len(bufs) + chunks
     return pl.pallas_call(
-        functools.partial(carry_kernel, REQUESTS),
+        carry_kernel,
         out_shape=[
-            jax.ShapeDtypeStruct((2 * CHUNKS, REQUESTS, *item), store.dtype),
+            jax.ShapeDtypeStruct((2 * chunks, REQUESTS, *item), store.dtype),
             jax.ShapeDtypeStruct((planes, RING_Y * RING_Z, *item), store.dtype),
         ],
         in_specs=[pl.BlockSpec(memory_space=pltpu.SMEM)] + [pl.BlockSpec(memory_space=pl.ANY)] * 2,
         out_specs=[pl.BlockSpec(memory_space=pltpu.VMEM)] * 2,
-        scratch_shapes=[pltpu.VMEM((2 * spans, rows // 2, enc_width), store.dtype)]
+        scratch_shapes=[pltpu.VMEM((2 * spans, *item), store.dtype)] * 2
         + bufs * 2
         + [
-            pltpu.VMEM((CHUNKS, REQUESTS, *item), store.dtype),
-            pltpu.SemaphoreType.DMA((4,)),
+            pltpu.VMEM((chunks, REQUESTS, *item), store.dtype),
+            pltpu.SemaphoreType.DMA((7,)),
             pltpu.SemaphoreType.DMA((copies,)),
             pltpu.SemaphoreType.DMA((copies,)),
             pltpu.SemaphoreType.DMA((13,)),
@@ -698,7 +705,7 @@
         )
 
     pieces = lax.cond(
-        worst[0, len(WIDTHS) + 2] > 0, resend, lambda store, ids, fast: fast, neighbour_store, neighbour_ids, pieces
+        worst[0, len(TRIPS) * COLUMNS] > 0, resend, lambda store, ids, fast: fast, neighbour_store, neighbour_ids, pieces
     )
     attended, best = attend(pieces, weight_own, key_slab, all_asked, attn_queries)
     column = (position // CORES) * 16

time: 284 us -> 239 us (0.84)
  Pallas kernels: 254 us -> 209 us
    pallas_call x1, Pallas kernels: 201 us -> 153 us  [carry(): pl.pallas_call(carry_kernel, out_shape=[jax.ShapeDtypeStruct((2 * chunks,...]
  transfers between devices with their start and end apart: 4 -> 4, of which waited for: 0 -> 0; matrix products, arithmetic and copies ran while one was open for 2% -> 2% of each run, Pallas kernels for 80% -> 76%
where the time goes in v3:
time: 239 us; the launch traced here: 238 us
  Pallas kernels  209 us (87%)
  between operations  14.8 us (6%)
  local copies, waits for them, and re-layouts  10.2 us (4%)
  starting transfers between devices  3.64 us (2%)
    pallas_call x1, Pallas kernels, carry(): pl.pallas_call(carry_kernel, out_shape=[jax.ShapeDtypeStruct((2 * chunks,...  153 us
    pallas_call x1, Pallas kernels, attend(): pl.pallas_call(attend_kernel, grid=(steps,), out_shape=[jax.ShapeDtypeStr...  28.6 us
    pallas_call x1, Pallas kernels, gather_ids(): pl.pallas_call(gather_ids_kernel, out_shape=jax.ShapeDtypeStruct(shape, j...  20.2 us
    pallas_call x1, Pallas kernels, routes(): pl.pallas_call(routes_kernel, out_shape=jax.ShapeDtypeStruct((2 * max(WID...  6.33 us
  transfers between devices with their start and end apart: 4, of which 0 were waited for; matrix products, arithmetic and copies ran while one was open for 2% of the time, Pallas kernels for 76%

profile of v3, /device:TPU:1, one launch (start us, length us, event | category | flops | bytes accessed | tf_op | source)
XLA Modules:
  0.0 238.1 jit_solution(7391621356898469016)
XLA Ops:
  7.2 0.0 all-gather.2.cloned.1.call-start
  7.2 1.3 pad.9
  8.5 0.0 all-gather.2.cloned.1.call-update
  8.5 0.8 copy.19
  9.3 0.1 reshape.167
  9.4 0.6 pad.8.ids_ref
  10.0 20.2 %gather_ids.1 = s32[4,8,2,8,128]{4,3,2,1,0:T(8,128)} custom-call(s32[8,128]{1,0:T(8,128)} %pad.8.ids_ref), custom_call_target="tpu_custom_call" | custom-call | tf_op jit(solution)/shard_map/gather_ids/pallas_call | solution.py:100
  30.2 1.1 slice_reduce_fusion
  31.2 0.7 reshape_squeeze.3.ids_ref
  32.0 6.3 %routes.1.table_ref = s32[48,128]{1,0:T(8,128)} custom-call(s32[1,768]{1,0:T(1,128)} %reshape_squeeze.3.ids_ref), custom_call_target="tpu_custom_call" | custom-call | tf_op jit(solution)/shard_map/routes/pallas_call | solution.py:469
  38.3 0.7 slice.40
  39.0 2.5 %collective-permute-start.2 = (s32[8,128]{1,0:T(8,128)S(1)}, s32[8,128]{1,0:T(8,128)S(1)}, u32[]{:S(2)}, u32[]{:S(2)}) collective-permute-start(s32[8,128]{1,0:T(8,128)S(1)} %slice.40), channel_id=1, source_target_pairs={{0,3},{1,0},{2,1},{3,2},{4,7},{5,4},{6,5},{7,6},{8,11},{9,8},{10,9... | collective-permute-start | bytes 12296 | tf_op jit(solution)/shard_map/ppermute | solution.py:694
  41.5 0.5 collective-permute-start.1
  42.0 0.6 collective-permute-start
  42.6 0.0 copy-start.5
  42.6 153.4 %carry.1 = (bf16[8,12,16,896]{3,2,1,0:T(8,128)(2,1)}, bf16[4,32,16,896]{3,2,1,0:T(8,128)(2,1)}) custom-call(s32[48,128]{1,0:T(8,128)} %routes.1.table_ref, bf16[64,64,896]{2,1,0:T(8,128)(2,1)} %store_ref.1, bf16[2,32,896]{2,1,0:T(8,128)(2,1)} %kv_ref.1), custom_call_target="tpu_custom_call" | custom-call | bytes 524288000 | tf_op jit(solution)/shard_map/carry/pallas_call | solution.py:634
  196.0 0.0 collective-permute-done.2
  196.0 0.0 collective-permute-done.1
  196.1 0.0 collective-permute-done
  196.1 0.7 maximum_maximum_fusion
  196.8 0.6 slice.38
  198.0 0.0 copy-done.5
  198.0 0.0 copy-start.2
  198.0 0.0 copy-start.4
  198.0 0.2 conditional.1
  198.2 0.0 all-gather.2.cloned.1.call-done
  198.3 1.2 copy-done.2
  199.4 0.0 copy-done.4
  199.4 0.0 copy-start.3
  199.4 1.4 copy-done.3
  200.8 28.6 %attend.1 = (bf16[384,2048]{1,0:T(8,128)(2,1)S(1)}, f32[8,512]{1,0:T(8,128)S(1)}) custom-call(bf16[8,12,16,896]{3,2,1,0:T(8,128)(2,1)} %get-tuple-element.42.pieces, bf16[4,32,16,896]{3,2,1,0:T(8,128)(2,1)} %get-tuple-element.21.w_own.w_all, bf16[4,32,16,896]{3,2,1,0:T(8,128)(2,1)} %get-tuple-element.21.w_own.w_all, bf16[64,768]{1,0:T(8,128)(2,1)S(1)} %copy-done.4, ...), custom_call_target="tpu_custom_call" | custom-call | flops 11274289152 | bytes 20971520 | tf_op jit(solution)/shard_map/attend/pallas_call | solution.py:343
  229.5 0.1 constant_dynamic-slice_fusion
  229.5 0.6 slice_bitcast_fusion
  230.1 1.1 copy.31
Async XLA Ops:
  7.2 191.1 %all-gather.2.cloned.1.call-start = ((), (), s32[]{:S(2)}) async-start(), calls=%async_computation.3 | async-start | bytes 1597440 | tf_op jit(solution)/shard_map/all_gather | solution.py:686
  39.0 157.1 %collective-permute-start.2 = (s32[8,128]{1,0:T(8,128)S(1)}, s32[8,128]{1,0:T(8,128)S(1)}, u32[]{:S(2)}, u32[]{:S(2)}) collective-permute-start(s32[8,128]{1,0:T(8,128)S(1)} %slice.40), channel_id=1, source_target_pairs={{0,3},{1,0},{2,1},{3,2},{4,7},{5,4},{6,5},{7,6},{8,11},{9,8},{10,9... | collective-permute-start | bytes 12296 | tf_op jit(solution)/shard_map/ppermute | solution.py:694
  41.5 154.6 %collective-permute-start.1 = (s32[8,128]{1,0:T(8,128)S(1)}, s32[8,128]{1,0:T(8,128)S(1)}, u32[]{:S(2)}, u32[]{:S(2)}) collective-permute-start(s32[8,128]{1,0:T(8,128)S(1)} %slice.40), channel_id=1, source_target_pairs={{0,2},{1,3},{2,0},{3,1},{4,6},{5,7},{6,4},{7,5},{8,10},{9,11},{10,... | collective-permute-start | bytes 12296 | tf_op jit(solution)/shard_map/ppermute | solution.py:694
  42.0 154.1 %collective-permute-start = (s32[8,128]{1,0:T(8,128)S(1)}, s32[8,128]{1,0:T(8,128)S(1)}, u32[]{:S(2)}, u32[]{:S(2)}) collective-permute-start(s32[8,128]{1,0:T(8,128)S(1)} %slice.40), channel_id=1, source_target_pairs={{0,1},{1,2},{2,3},{3,0},{4,5},{5,6},{6,7},{7,4},{8,9},{9,10},{10,1... | collective-permute-start | bytes 12296 | tf_op jit(solution)/shard_map/ppermute | solution.py:694
  42.6 155.4 %copy-start.5 = (s32[6,2]{0,1:T(2,128)S(1)}, s32[6,2]{0,1:T(2,128)}, u32[]{:S(2)}) copy-start(s32[6,2]{0,1:T(2,128)} %param.11) | copy-start | bytes 148
  198.0 1.4 copy-start.2
  198.0 1.4 copy-start.4
  199.4 1.4 copy-start.3
Sparse Core Ops, SparseCore 0:
  10.7 82.9 all-gather.1

commit v4 on v3

--- a/solution.py
+++ b/solution.py
@@ -71,46 +71,56 @@
     return copy
 
 
-def gather_ids_kernel(ids_ref, out_ref, held, send_sem, recv_sem):
+def gather_ids_kernel(ids_ref, store_ref, out_ref, swapped_ref, held, rows, send_sem, recv_sem):
     y, z, c = place()
     core, depth, row = peer_groups()
     greet(core + depth + row)
-    held[y, z, c] = ids_ref[...]
-    copies = [send(held.at[y, z, c], held.at[y, z, c], send_sem.at[0], recv_sem.at[0], core[0])]
+    held[z, c] = ids_ref[...]
+    own = held.at[z, c]
+    first = send(own, own, send_sem.at[0], recv_sem.at[0], core[0])
+    half = swapped_ref.shape[1]
+    theirs = pl.ds(pl.multiple_of((1 - c) * half, half), half)
+    swap = send(store_ref.at[:, theirs], swapped_ref, send_sem.at[11], recv_sem.at[11], core[0])
+    first.wait()
+    copies = []
+    for i, peer in enumerate(depth):
+        copies.append(send(held.at[z], held.at[z], send_sem.at[1 + i], recv_sem.at[1 + i], peer))
     for copy in copies:
         copy.wait()
+    rows[y] = held[:, :, 0, :].reshape(rows.shape[1:])
     copies = []
-    for i, peer in enumerate(depth):
-        copies.append(
-            send(held.at[y, z], held.at[y, z], send_sem.at[1 + i], recv_sem.at[1 + i], peer)
-        )
+    for i, peer in enumerate(row):
+        copies.append(send(rows.at[y], rows.at[y], send_sem.at[8 + i], recv_sem.at[8 + i], peer))
     for copy in copies:
         copy.wait()
-    copies = []
-    for i, peer in enumerate(row):
-        copies.append(send(held.at[y], held.at[y], send_sem.at[8 + i], recv_sem.at[8 + i], peer))
-    for copy in copies:
-        copy.wait()
-    out_ref[...] = held[...]
-
-
-def gather_ids(ids):
+    out_ref[...] = rows[...]
+    swap.wait()
+
+
+def gather_ids(ids, store):
     tile = jnp.pad(ids.reshape(1, -1), ((0, 7), (0, 128 - ids.size)))
-    shape = (RING_Y, RING_Z, CORES, 8, 128)
-    held = pl.pallas_call(
+    shape = (RING_Y, RING_Z * CORES, 128)
+    spans, span_rows, width = store.shape
+    all_ids, swapped = pl.pallas_call(
         gather_ids_kernel,
-        out_shape=jax.ShapeDtypeStruct(shape, jnp.int32),
-        in_specs=[pl.BlockSpec(memory_space=pltpu.VMEM)],
-        out_specs=pl.BlockSpec(memory_space=pltpu.VMEM),
+        out_shape=[
+            jax.ShapeDtypeStruct(shape, jnp.int32),
+            jax.ShapeDtypeStruct((spans, span_rows // 2, width), store.dtype),
+        ],
+        in_specs=[pl.BlockSpec(memory_space=pltpu.VMEM), pl.BlockSpec(memory_space=pl.ANY)],
+        out_specs=[pl.BlockSpec(memory_space=pltpu.VMEM)] * 2,
         scratch_shapes=[
+            pltpu.VMEM((RING_Z, CORES, 8, 128), jnp.int32),
             pltpu.VMEM(shape, jnp.int32),
-            pltpu.SemaphoreType.DMA((11,)),
-            pltpu.SemaphoreType.DMA((11,)),
+            pltpu.SemaphoreType.DMA((12,)),
+            pltpu.SemaphoreType.DMA((12,)),
         ],
-        compiler_params=pltpu.CompilerParams(collective_id=0, has_side_effects=True),
+        compiler_params=pltpu.CompilerParams(
+            collective_id=0, has_side_effects=True, vmem_limit_bytes=60 << 20
+        ),
         name="gather_ids",
-    )(tile)
-    return held[..., 0, : ids.size].reshape(1, -1)
+    )(tile, store)
+    return all_ids.reshape(-1, 128)[:, : ids.size].reshape(1, -1), swapped
 
 
 def merge(a, b):
@@ -371,7 +381,7 @@
             pltpu.SemaphoreType.DMA((19,)),
         ],
         compiler_params=pltpu.CompilerParams(
-            collective_id=1, has_side_effects=True, vmem_limit_bytes=48 << 20
+            collective_id=1, has_side_effects=True, vmem_limit_bytes=60 << 20
         ),
         cost_estimate=pl.CostEstimate(
             flops=flops, bytes_accessed=20 << 20, transcendentals=tokens * HEADS * 256
@@ -483,31 +493,51 @@
 )
 
 
-def carry_kernel(table_ref, store_ref, kv_ref, out_ref, w_ref, *rest):
+def carry_kernel(table_ref, flag_ref, store_ref, swapped_ref, kv_ref, out_ref, w_ref, worst_ref, *rest):
     rounds = len(MOVES[0])
     total = len(CHUNK_TRIPS) * rounds
     held, rest = rest[:2], rest[2:]
     out_bufs = rest[:total]
     in_bufs = rest[total : 2 * total]
-    last, swap_sems, send_sems, recv_sems, w_send_sems, w_recv_sems = rest[2 * total :]
+    last, flags, held_sems, send_sems, recv_sems, w_send_sems, w_recv_sems = rest[2 * total :]
     y, z, c = place()
     spans = store_ref.shape[0]
     steps = [((y + dy) % RING_Y, (z + dz) % RING_Z) for dy, dz in ((1, 0), (-1, 0), (0, 1), (0, -1))]
     near = [key_of(a, b, c) for a, b in steps]
     buddy = key_of(y, z, 1 - c)
+    halves = {}
+    for part in (1, 0):
+        mine = pl.ds(pl.multiple_of((2 * c + part) * PART, PART), PART)
+        halves[part] = [
+            pltpu.make_async_copy(
+                store_ref.at[:, mine], held[part].at[pl.ds(0, spans)], held_sems.at[2 * part]
+            ),
+            pltpu.make_async_copy(
+                swapped_ref.at[:, pl.ds(part * PART, PART)],
+                held[part].at[pl.ds(spans, spans)],
+                held_sems.at[2 * part + 1],
+            ),
+        ]
+        for copy in halves[part]:
+            copy.start()
     _, depth, row = peer_groups()
     x, planes = lax.axis_index("seq"), lax.axis_size("seq")
     seq = [lax.rem(x + d, planes) for d in range(1, planes)]
     greet(depth + row + [buddy], seq)
     quarter = kv_ref.at[x // 2, pl.ds(pl.multiple_of((x % 2) * PART, PART), PART)]
     pair = y * RING_Z + z
-    own = pltpu.make_async_copy(quarter, w_ref.at[x, pair], swap_sems.at[6])
+    own = pltpu.make_async_copy(quarter, w_ref.at[x, pair], held_sems.at[4])
     own.start()
     w_flights = [
         [
             send(quarter, w_ref.at[x, pair], w_send_sems.at[i], w_recv_sems.at[i], peer)
             for i, peer in enumerate(depth)
         ]
+    ]
+
+    flag_flights = [
+        send(flag_ref.at[pl.ds(0, 8)], flags.at[i], w_send_sems.at[13 + i], w_recv_sems.at[13 + i], peer, "seq")
+        for i, peer in enumerate(seq)
     ]
 
     def pass_on(stage):
@@ -526,22 +556,6 @@
             ]
         )
 
-    halves = {}
-    for part in (1, 0):
-        mine = pl.ds(pl.multiple_of((2 * c + part) * PART, PART), PART)
-        theirs = pl.ds(pl.multiple_of((2 * (1 - c) + part) * PART, PART), PART)
-        keep = pltpu.make_async_copy(
-            store_ref.at[:, mine], held[part].at[pl.ds(0, spans)], swap_sems.at[3 * part + 2]
-        )
-        keep.start()
-        swap = send(
-            store_ref.at[:, theirs],
-            held[part].at[pl.ds(spans, spans)],
-            swap_sems.at[3 * part],
-            swap_sems.at[3 * part + 1],
-            buddy,
-        )
-        halves[part] = (swap, keep)
     ready = set()
     bases = [
         np.concatenate([[2 * spans], 2 * spans + np.cumsum(2 * np.array(w))]).tolist() for w in WIDTHS
@@ -619,12 +633,17 @@
         land(j, rounds)
     for copy in w_flights[-1]:
         copy.wait_recv()
-    for copies in list(flights.values()) + w_flights:
+    worst = flag_ref[0:8, :]
+    for i, copy in enumerate(flag_flights):
+        copy.wait_recv()
+        worst = jnp.maximum(worst, flags[i])
+    worst_ref[...] = worst
+    for copies in list(flights.values()) + w_flights + [flag_flights]:
         for copy in copies:
             copy.wait_send()
 
 
-def carry(store, kv_weight, table):
+def carry(store, swapped, kv_weight, table):
     spans, _, enc_width = store.shape
     planes = lax.axis_size("seq")
     item = (PART, enc_width)
@@ -636,25 +655,28 @@
         out_shape=[
             jax.ShapeDtypeStruct((2 * chunks, REQUESTS, *item), store.dtype),
             jax.ShapeDtypeStruct((planes, RING_Y * RING_Z, *item), store.dtype),
+            jax.ShapeDtypeStruct((8, 128), table.dtype),
         ],
-        in_specs=[pl.BlockSpec(memory_space=pltpu.SMEM)] + [pl.BlockSpec(memory_space=pl.ANY)] * 2,
-        out_specs=[pl.BlockSpec(memory_space=pltpu.VMEM)] * 2,
+        in_specs=[pl.BlockSpec(memory_space=pltpu.SMEM), pl.BlockSpec(memory_space=pltpu.VMEM)]
+        + [pl.BlockSpec(memory_space=pl.ANY)] * 3,
+        out_specs=[pl.BlockSpec(memory_space=pltpu.VMEM)] * 3,
         scratch_shapes=[pltpu.VMEM((2 * spans, *item), store.dtype)] * 2
         + bufs * 2
         + [
             pltpu.VMEM((chunks, REQUESTS, *item), store.dtype),
-            pltpu.SemaphoreType.DMA((7,)),
+            pltpu.VMEM((planes - 1, 8, 128), table.dtype),
+            pltpu.SemaphoreType.DMA((5,)),
             pltpu.SemaphoreType.DMA((copies,)),
             pltpu.SemaphoreType.DMA((copies,)),
-            pltpu.SemaphoreType.DMA((13,)),
-            pltpu.SemaphoreType.DMA((13,)),
+            pltpu.SemaphoreType.DMA((16,)),
+            pltpu.SemaphoreType.DMA((16,)),
         ],
         compiler_params=pltpu.CompilerParams(
             collective_id=2, has_side_effects=True, vmem_limit_bytes=60 << 20
         ),
         cost_estimate=pl.CostEstimate(flops=0, bytes_accessed=500 << 20, transcendentals=0),
         name="carry",
-    )(table, store, kv_weight)
+    )(table, table, store, swapped, kv_weight)
 
 
 def direct(neighbour_store, neighbour_ids):
@@ -681,19 +703,12 @@
     y, z, c = place()
     own_spans = neighbour_ids.shape[0]
     span_rows = neighbour_store.shape[1]
-    all_ids = gather_ids(neighbour_ids)
+    all_ids, swapped = gather_ids(neighbour_ids, neighbour_store)
     asked = jnp.pad(span_queries, ((0, 16 - own_spans), (0, 0)))
     all_asked = lax.all_gather(asked, "keys", axis=0, tiled=True)
     all_asked = all_asked.reshape(RING_Y * RING_Z, CORES, *asked.shape)
     table = routes(all_ids)
-    flag = table[:8]
-    seq = lax.axis_size("seq")
-    worst = flag
-    for d in range(1, seq):
-        worst = jnp.maximum(
-            worst, lax.ppermute(flag, "seq", [(s, (s + d) % seq) for s in range(seq)])
-        )
-    pieces, weight_own = carry(neighbour_store, kv_weight, table)
+    pieces, weight_own, worst = carry(neighbour_store, swapped, kv_weight, table)
 
     def resend(store, ids, fast):
         return jnp.stack(

time: 239 us -> 231 us (0.967)
  starting transfers between devices: 3.64 us -> 0.04 us
  Pallas kernels: 209 us -> 206 us
    ppermute x3 -> x0, starting transfers between devices: 3.6 us -> none  [body(): lax.ppermute(flag, 'seq', [(s, (s + d) % seq) for s in range(seq)])]
    pallas_call x1, Pallas kernels: 153 us -> 150 us  [carry(): pl.pallas_call(carry_kernel, out_shape=[jax.ShapeDtypeStruct((2 * chunks,...]
  transfers between devices with their start and end apart: 4 -> 1, of which waited for: 0 -> 0; matrix products, arithmetic and copies ran while one was open for 2% -> 2% of each run, Pallas kernels for 76% -> 77%
where the time goes in v4:
time: 231 us; the launch traced here: 230 us
  Pallas kernels  206 us (89%)
  between operations  14.8 us (6%)
  local copies, waits for them, and re-layouts  9.53 us (4%)
    pallas_call x1, Pallas kernels, carry(): pl.pallas_call(carry_kernel, out_shape=[jax.ShapeDtypeStruct((2 * chunks,...  150 us
    pallas_call x1, Pallas kernels, attend(): pl.pallas_call(attend_kernel, grid=(steps,), out_shape=[jax.ShapeDtypeStr...  29.4 us
    pallas_call x1, Pallas kernels, gather_ids(): pl.pallas_call(gather_ids_kernel, out_shape=[jax.ShapeDtypeStruct(shape,...  19.7 us
    pallas_call x1, Pallas kernels, routes(): pl.pallas_call(routes_kernel, out_shape=jax.ShapeDtypeStruct((2 * max(WID...  6.34 us
  transfers between devices with their start and end apart: 1, of which 0 were waited for; matrix products, arithmetic and copies ran while one was open for 2% of the time, Pallas kernels for 77%

profile of v4, /device:TPU:1, one launch (start us, length us, event | category | flops | bytes accessed | tf_op | source)
XLA Modules:
  0.0 230.4 jit_solution(3420184576647004080)
XLA Ops:
  7.2 0.0 all-gather.2.cloned.1.call-start
  7.2 1.3 pad.9
  8.5 0.0 all-gather.2.cloned.1.call-update
  8.6 0.8 copy.19
  9.3 0.1 reshape.173
  9.4 0.6 pad.8.ids_ref
  10.0 19.7 %gather_ids.1 = (s32[4,16,128]{2,1,0:T(8,128)}, bf16[64,32,896]{2,1,0:T(8,128)(2,1)}) custom-call(s32[8,128]{1,0:T(8,128)} %pad.8.ids_ref, bf16[64,64,896]{2,1,0:T(8,128)(2,1)} %store_ref.3), custom_call_target="tpu_custom_call" | custom-call | tf_op jit(solution)/shard_map/gather_ids/pallas_call | solution.py:104
  29.7 1.5 reshape.175.ids_ref
  31.2 6.3 %routes.1.table_ref.flag_ref = s32[48,128]{1,0:T(8,128)} custom-call(s32[1,768]{1,0:T(1,128)} %reshape.175.ids_ref), custom_call_target="tpu_custom_call" | custom-call | tf_op jit(solution)/shard_map/routes/pallas_call | solution.py:479
  37.5 0.0 copy-start.2
  37.5 150.4 %carry.1 = (bf16[8,12,16,896]{3,2,1,0:T(8,128)(2,1)}, bf16[4,32,16,896]{3,2,1,0:T(8,128)(2,1)}, s32[8,128]{1,0:T(8,128)}) custom-call(s32[48,128]{1,0:T(8,128)} %routes.1.table_ref.flag_ref, s32[48,128]{1,0:T(8,128)} %routes.1.table_ref.flag_ref, bf16[64,64,896]{2,1,0:T(8,128)(2,1)} %store_ref.3, bf16[64,32,896]{2,1,0:T(8,128)(2,1)} %get-tuple-element.24.swapped_ref, ...), custom_call_target="tpu_custom_call" | custom-call | bytes 524288000 | tf_op jit(solution)/shard_map/carry/pallas_call | solution.py:653
  187.9 1.3 slice.34
  189.9 0.0 copy-done.2
  189.9 0.2 conditional.1
  190.1 0.0 all-gather.2.cloned.1.call-done
  190.1 29.4 %attend.1 = (bf16[384,2048]{1,0:T(8,128)(2,1)}, f32[8,512]{1,0:T(8,128)}) custom-call(bf16[8,12,16,896]{3,2,1,0:T(8,128)(2,1)} %get-tuple-element.48.pieces, bf16[4,32,16,896]{3,2,1,0:T(8,128)(2,1)} %get-tuple-element.27.w_own.w_all, bf16[4,32,16,896]{3,2,1,0:T(8,128)(2,1)} %get-tuple-element.27.w_own.w_all, bf16[64,768]{1,0:T(8,128)(2,1)} %slab.1, ...), custom_call_target="tpu_custom_call" | custom-call | flops 11274289152 | bytes 20971520 | tf_op jit(solution)/shard_map/attend/pallas_call | solution.py:353
  219.5 0.8 constant_dynamic-slice_fusion
  220.3 0.6 slice_bitcast_fusion
  220.8 2.7 %copy.31 = bf16[384,2048]{1,0:T(8,128)(2,1)} copy(bf16[384,2048]{1,0:T(8,128)(2,1)} %get-tuple-element.47) | data formatting | bytes 3145728
Async XLA Ops:
  7.2 182.9 %all-gather.2.cloned.1.call-start = ((), (), s32[]{:S(2)}) async-start(), calls=%async_computation.3 | async-start | bytes 1597440 | tf_op jit(solution)/shard_map/all_gather | solution.py:708
  37.5 152.3 %copy-start.2 = (s32[6,2]{0,1:T(2,128)S(1)}, s32[6,2]{0,1:T(2,128)}, u32[]{:S(2)}) copy-start(s32[6,2]{0,1:T(2,128)} %param.11) | copy-start | bytes 148
Sparse Core Ops, SparseCore 0:
  10.7 82.5 all-gather.1

commit v5 on v4

--- a/solution.py
+++ b/solution.py
@@ -11,7 +11,7 @@
 HEADS = 16
 HEAD_DIM = 128
 RING_Y, RING_Z, CORES = 4, 8, 2
-Y_CAPS, Z_CAPS = (24, 17), (12, 12, 11, 10)
+Y_CAPS, Z_CAPS = (24, 17), (12, 11, 10, 10)
 Z_FIRST_CAPS, Y_LAST_CAPS = (19, 16, 16, 15), (14, 11)
 TRIPS = (((True, Y_CAPS), (False, Z_CAPS)), ((False, Z_FIRST_CAPS), (True, Y_LAST_CAPS)))
 MOVES = tuple([along for along, caps in trip for _ in caps] for trip in TRIPS)
@@ -381,7 +381,7 @@
             pltpu.SemaphoreType.DMA((19,)),
         ],
         compiler_params=pltpu.CompilerParams(
-            collective_id=1, has_side_effects=True, vmem_limit_bytes=60 << 20
+            collective_id=1, has_side_effects=True, vmem_limit_bytes=48 << 20
         ),
         cost_estimate=pl.CostEstimate(
             flops=flops, bytes_accessed=20 << 20, transcendentals=tokens * HEADS * 256

time: 231 us -> 226 us (0.978)
  Pallas kernels: 206 us -> 201 us
    pallas_call x1, Pallas kernels: 150 us -> 147 us  [carry(): pl.pallas_call(carry_kernel, out_shape=[jax.ShapeDtypeStruct((2 * chunks,...]
where the time goes in v5:
time: 226 us
  Pallas kernels  201 us (89%)
  between operations  14.8 us (7%)
  local copies, waits for them, and re-layouts  9.85 us (4%)
    pallas_call x1, Pallas kernels, carry(): pl.pallas_call(carry_kernel, out_shape=[jax.ShapeDtypeStruct((2 * chunks,...  147 us
    pallas_call x1, Pallas kernels, attend(): pl.pallas_call(attend_kernel, grid=(steps,), out_shape=[jax.ShapeDtypeStr...  28.1 us
    pallas_call x1, Pallas kernels, gather_ids(): pl.pallas_call(gather_ids_kernel, out_shape=[jax.ShapeDtypeStruct(shape,...  19.7 us
    pallas_call x1, Pallas kernels, routes(): pl.pallas_call(routes_kernel, out_shape=jax.ShapeDtypeStruct((2 * max(WID...  6.35 us
  transfers between devices with their start and end apart: 1, of which 0 were waited for; matrix products, arithmetic and copies ran while one was open for 2% of the time, Pallas kernels for 77%

profile of v5, /device:TPU:1, one launch (start us, length us, event | category | flops | bytes accessed | tf_op | source)
XLA Modules:
  0.0 225.7 jit_solution(9032132449280789617)
XLA Ops:
  7.2 0.0 all-gather.2.cloned.1.call-start
  7.2 1.3 pad.9
  8.5 0.0 all-gather.2.cloned.1.call-update
  8.6 0.8 copy.19
  9.3 0.1 reshape.173
  9.4 0.6 pad.8.ids_ref
  10.0 19.7 %gather_ids.1 = (s32[4,16,128]{2,1,0:T(8,128)}, bf16[64,32,896]{2,1,0:T(8,128)(2,1)}) custom-call(s32[8,128]{1,0:T(8,128)} %pad.8.ids_ref, bf16[64,64,896]{2,1,0:T(8,128)(2,1)} %store_ref.3), custom_call_target="tpu_custom_call" | custom-call | tf_op jit(solution)/shard_map/gather_ids/pallas_call | solution.py:104
  29.7 1.5 reshape.175.ids_ref
  31.2 6.3 %routes.1.table_ref.flag_ref = s32[48,128]{1,0:T(8,128)} custom-call(s32[1,768]{1,0:T(1,128)} %reshape.175.ids_ref), custom_call_target="tpu_custom_call" | custom-call | tf_op jit(solution)/shard_map/routes/pallas_call | solution.py:479
  37.5 0.0 copy-start.5
  37.5 146.7 %carry.1 = (bf16[8,12,16,896]{3,2,1,0:T(8,128)(2,1)}, bf16[4,32,16,896]{3,2,1,0:T(8,128)(2,1)}, s32[8,128]{1,0:T(8,128)}) custom-call(s32[48,128]{1,0:T(8,128)} %routes.1.table_ref.flag_ref, s32[48,128]{1,0:T(8,128)} %routes.1.table_ref.flag_ref, bf16[64,64,896]{2,1,0:T(8,128)(2,1)} %store_ref.3, bf16[64,32,896]{2,1,0:T(8,128)(2,1)} %get-tuple-element.24.swapped_ref, ...), custom_call_target="tpu_custom_call" | custom-call | bytes 524288000 | tf_op jit(solution)/shard_map/carry/pallas_call | solution.py:653
  184.2 1.3 slice.34
  186.2 0.0 copy-done.5
  186.2 0.0 copy-start.2
  186.2 0.0 copy-start.4
  186.2 0.2 conditional.1
  186.4 0.0 all-gather.2.cloned.1.call-done
  186.4 1.2 copy-done.2
  187.6 0.0 copy-done.4
  187.6 0.0 copy-start.3
  187.6 1.4 copy-done.3
  189.0 28.1 %attend.1 = (bf16[384,2048]{1,0:T(8,128)(2,1)S(1)}, f32[8,512]{1,0:T(8,128)S(1)}) custom-call(bf16[8,12,16,896]{3,2,1,0:T(8,128)(2,1)} %get-tuple-element.48.pieces, bf16[4,32,16,896]{3,2,1,0:T(8,128)(2,1)} %get-tuple-element.27.w_own.w_all, bf16[4,32,16,896]{3,2,1,0:T(8,128)(2,1)} %get-tuple-element.27.w_own.w_all, bf16[64,768]{1,0:T(8,128)(2,1)S(1)} %copy-done.4, ...), custom_call_target="tpu_custom_call" | custom-call | flops 11274289152 | bytes 20971520 | tf_op jit(solution)/shard_map/attend/pallas_call | solution.py:353
  217.1 0.1 constant_dynamic-slice_fusion
  217.2 0.6 slice_bitcast_fusion
  217.8 1.1 copy.31
Async XLA Ops:
  7.2 179.2 %all-gather.2.cloned.1.call-start = ((), (), s32[]{:S(2)}) async-start(), calls=%async_computation.3 | async-start | bytes 1597440 | tf_op jit(solution)/shard_map/all_gather | solution.py:708
  37.5 148.6 %copy-start.5 = (s32[6,2]{0,1:T(2,128)S(1)}, s32[6,2]{0,1:T(2,128)}, u32[]{:S(2)}) copy-start(s32[6,2]{0,1:T(2,128)} %param.11) | copy-start | bytes 148
  186.2 1.4 copy-start.2
  186.2 1.4 copy-start.4
  187.6 1.4 copy-start.3
Sparse Core Ops, SparseCore 0:
  10.7 82.5 all-gather.1
